TPU v7x, 512 devices: a whole 4x4x16 slice. The times are simulated.
512 devices in a mesh: seq: 8 (over y, core), fsdp: 16 (over z), dp: 4 (over x).
Axes of the slice: x: 4, y: 4, z: 16, core: 2. Of those that a mesh axis runs over, the one named last changes fastest.
Arguments:
- query_in: bfloat16 [64, 1024, 1536], P(('fsdp', 'dp'), 'seq'), may hold values from -8 to 8
- key_in: bfloat16 [64, 1024, 1536], P(('fsdp', 'dp'), 'seq'), may hold values from -8 to 8
- value_in: bfloat16 [64, 1024, 1536], P(('fsdp', 'dp'), 'seq'), may hold values from -24 to 24
- out_grad: bfloat16 [64, 1024, 1536], P(('fsdp', 'dp'), 'seq'), may hold values from -16 to 16
- out_weight: bfloat16 [1536, 1536], P('seq', 'fsdp'), may hold values from -0.15625 to 0.15625
- key_tiles: int32 [64, 24, 32, 6], P(('fsdp', 'dp'), 'seq'), may hold values from 0 to 31, as said below
- key_count: int32 [64, 24, 32], P(('fsdp', 'dp'), 'seq'), may hold values from 1 to 6, as said below
Outputs:
- layer_out: bfloat16 [64, 1024, 1536], P(('fsdp', 'dp'), 'seq')
- query_grad: bfloat16 [64, 1024, 1536], P(('fsdp', 'dp'), 'seq')
- key_grad: bfloat16 [64, 1024, 1536], P(('fsdp', 'dp'), 'seq')
- value_grad: bfloat16 [64, 1024, 1536], P(('fsdp', 'dp'), 'seq')
- weight_grad: float32 [1536, 1536], P('seq', ('fsdp', 'dp'))
Inputs may be any that keep to these rules, and one draw needn't show every extreme that they name: Tile m lies in frame m // 2, row (m) % 2 and column m % 1 of a grid of 16 frames. The first key_count[c, h, n] entries of key_tiles[c, h, n, :] are, in some order, the distinct tiles whose frame, row and column differ from those of tile n by at most the frame, row and column reach of head h in clip c, each 0 or 1; the remaining entries are arbitrary tile numbers. `key_count`: the number of live entries of each list; every clip has a list with 6.
All inputs are finite; a program needn't handle non-finite values.
Results may differ from a plain program's by a relative error of at most 0.02.
Values may be sent and summed in bfloat16 or wider, within the bound.
No kernel may reach another device: no remote copies, remote signals or barrier semaphores. Data moves between devices by JAX's collectives and lax.ppermute only.
A program may use at most 128 MiB of HBM per device.

v0:
```python
import jax
import jax.numpy as jnp
from jax import lax
from jax.sharding import PartitionSpec as P


def head_forward(query_head, key_head, value_head, head_list, tile_counts):
    tile_number, tile_len, head_dim = query_head.shape
    slot_number = head_list.shape[1]
    score_scale = head_dim ** (-0.5)
    key_chosen = key_head[head_list].reshape(tile_number, slot_number * tile_len, head_dim)
    value_chosen = value_head[head_list].reshape(tile_number, slot_number * tile_len, head_dim)
    kept_mask = (jnp.arange(slot_number * tile_len) // tile_len)[None, :] < tile_counts[:, None]
    scores = (
        jnp.einsum("nqd,nkd->nqk", query_head, key_chosen, preferred_element_type=jnp.float32)
        * score_scale
    )
    scores = jnp.where(kept_mask[:, None, :], scores, -jnp.inf)
    row_max = jnp.max(scores, axis=-1, keepdims=True)
    log_total = row_max + jnp.log(jnp.sum(jnp.exp(scores - row_max), axis=-1, keepdims=True))
    rounded = jnp.exp(scores - log_total).astype(jnp.bfloat16)
    attended = jnp.einsum(
        "nqk,nkd->nqd", rounded, value_chosen, preferred_element_type=jnp.float32
    ).astype(jnp.bfloat16)
    return (attended, log_total)


def head_backward(
    query_head, key_head, value_head, head_list, tile_counts, attended, log_total, upstream
):
    tile_number, tile_len, head_dim = query_head.shape
    slot_number = head_list.shape[1]
    score_scale = head_dim ** (-0.5)
    key_chosen = key_head[head_list].reshape(tile_number, slot_number * tile_len, head_dim)
    value_chosen = value_head[head_list].reshape(tile_number, slot_number * tile_len, head_dim)
    kept_mask = (jnp.arange(slot_number * tile_len) // tile_len)[None, :] < tile_counts[:, None]
    scores = (
        jnp.einsum("nqd,nkd->nqk", query_head, key_chosen, preferred_element_type=jnp.float32)
        * score_scale
    )
    scores = jnp.where(kept_mask[:, None, :], scores, -jnp.inf)
    weights = jnp.exp(scores - log_total)
    rounded = weights.astype(jnp.bfloat16)
    inner_sum = jnp.sum(
        upstream.astype(jnp.float32) * attended.astype(jnp.float32), axis=-1, keepdims=True
    )
    prob_grad = jnp.einsum(
        "nqd,nkd->nqk", upstream, value_chosen, preferred_element_type=jnp.float32
    )
    score_grad = (weights * (prob_grad - inner_sum)).astype(jnp.bfloat16)
    query_grad = (
        jnp.einsum("nqk,nkd->nqd", score_grad, key_chosen, preferred_element_type=jnp.float32)
        * score_scale
    ).astype(jnp.bfloat16)
    key_slots = (
        jnp.einsum("nqk,nqd->nkd", score_grad, query_head, preferred_element_type=jnp.float32)
        * score_scale
    )
    value_slots = jnp.einsum("nqk,nqd->nkd", rounded, upstream, preferred_element_type=jnp.float32)
    live_slots = jnp.arange(slot_number)[None, :] < tile_counts[:, None]
    one_hot = (
        (head_list[:, :, None] == jnp.arange(tile_number)[None, None, :]) & live_slots[:, :, None]
    ).astype(jnp.float32)
    slot_shape = (tile_number, slot_number, tile_len, head_dim)
    key_grad = jnp.einsum(
        "nst,nsrd->trd", one_hot, key_slots.reshape(slot_shape), precision=lax.Precision.HIGHEST
    ).astype(jnp.bfloat16)
    value_grad = jnp.einsum(
        "nst,nsrd->trd", one_hot, value_slots.reshape(slot_shape), precision=lax.Precision.HIGHEST
    ).astype(jnp.bfloat16)
    return (query_grad, key_grad, value_grad)


def heads_to_rows(stacked):
    return jnp.transpose(stacked, (1, 2, 0, 3)).reshape(
        stacked.shape[1] * stacked.shape[2], stacked.shape[0] * stacked.shape[3]
    )


def pick_head(field, head_index):
    return lax.dynamic_index_in_dim(field, head_index, 2, keepdims=False)


def per_device(query_in, key_in, value_in, out_grad, out_weight, key_tiles, key_count):
    seq_size = lax.axis_size("seq")
    fsdp_size = lax.axis_size("fsdp")
    local_tokens = query_in.shape[1]
    query_heads, key_heads, value_heads = (
        lax.all_to_all(query_in[0], "seq", split_axis=1, concat_axis=0, tiled=True),
        lax.all_to_all(key_in[0], "seq", split_axis=1, concat_axis=0, tiled=True),
        lax.all_to_all(value_in[0], "seq", split_axis=1, concat_axis=0, tiled=True),
    )
    clip_lists = key_tiles[0]
    clip_counts = key_count[0]
    local_heads, tile_number, slot_number = clip_lists.shape
    all_tokens = query_heads.shape[0]
    tile_len = all_tokens // tile_number
    head_dim = query_heads.shape[1] // local_heads
    grid_shape = (tile_number, tile_len, local_heads, head_dim)
    query_grid = query_heads.reshape(grid_shape)
    key_grid = key_heads.reshape(grid_shape)
    value_grid = value_heads.reshape(grid_shape)

    def forward_head(head_index):
        return head_forward(
            pick_head(query_grid, head_index),
            pick_head(key_grid, head_index),
            pick_head(value_grid, head_index),
            clip_lists[head_index],
            clip_counts[head_index],
        )

    attended, log_total = lax.map(forward_head, jnp.arange(local_heads))
    attn_heads = heads_to_rows(attended)
    attn_tokens = lax.all_to_all(attn_heads, "seq", split_axis=0, concat_axis=1, tiled=True)
    row_block, col_block = out_weight.shape
    gathered = lax.all_gather(out_weight[None], ("seq", "fsdp"), axis=0, tiled=True)
    full_weight = gathered.reshape(seq_size, fsdp_size, row_block, col_block)
    weight_code = "sfrc"
    attn_split = attn_tokens.reshape(local_tokens, seq_size, row_block)
    layer_out = jnp.einsum(
        "tsr," + weight_code + "->tfc", attn_split, full_weight, preferred_element_type=jnp.float32
    )
    layer_out = layer_out.reshape(local_tokens, fsdp_size * col_block).astype(jnp.bfloat16)
    grad_all = lax.all_gather(out_grad[0], "seq", axis=0, tiled=True)
    grad_split = out_grad[0].reshape(local_tokens, fsdp_size, col_block)
    upstream_tokens = jnp.einsum(
        "tfc," + weight_code + "->tsr", grad_split, full_weight, preferred_element_type=jnp.float32
    )
    upstream_tokens = upstream_tokens.reshape(local_tokens, seq_size * row_block).astype(
        jnp.bfloat16
    )
    upstream = lax.all_to_all(upstream_tokens, "seq", split_axis=1, concat_axis=0, tiled=True)
    upstream_grid = upstream.reshape(grid_shape)

    def backward_head(head_index):
        return head_backward(
            pick_head(query_grid, head_index),
            pick_head(key_grid, head_index),
            pick_head(value_grid, head_index),
            clip_lists[head_index],
            clip_counts[head_index],
            attended[head_index],
            log_total[head_index],
            pick_head(upstream_grid, head_index),
        )

    query_back, key_back, value_back = lax.map(backward_head, jnp.arange(local_heads))
    query_grad, key_grad, value_grad = (
        lax.all_to_all(heads_to_rows(query_back), "seq", split_axis=0, concat_axis=1, tiled=True),
        lax.all_to_all(heads_to_rows(key_back), "seq", split_axis=0, concat_axis=1, tiled=True),
        lax.all_to_all(heads_to_rows(value_back), "seq", split_axis=0, concat_axis=1, tiled=True),
    )
    weight_term = lax.dot_general(
        attn_heads, grad_all, (((0,), (0,)), ((), ())), preferred_element_type=jnp.float32
    )
    weight_part = lax.psum_scatter(weight_term, ("fsdp", "dp"), scatter_dimension=1, tiled=True)
    weight_grad = weight_part / (fsdp_size * lax.axis_size("dp"))
    return (layer_out[None], query_grad[None], key_grad[None], value_grad[None], weight_grad)


def solution(mesh):
    placed = (
        P(("fsdp", "dp"), "seq", None),
        P(("fsdp", "dp"), "seq", None),
        P(("fsdp", "dp"), "seq", None),
        P(("fsdp", "dp"), "seq", None),
        P("seq", "fsdp"),
        P(("fsdp", "dp"), "seq", None, None),
        P(("fsdp", "dp"), "seq", None),
    )
    return jax.shard_map(
        per_device,
        mesh=mesh,
        in_specs=placed,
        out_specs=(
            P(("fsdp", "dp"), "seq", None),
            P(("fsdp", "dp"), "seq", None),
            P(("fsdp", "dp"), "seq", None),
            P(("fsdp", "dp"), "seq", None),
            P("seq", ("fsdp", "dp")),
        ),
        check_vma=False,
    )
```

profile of v0, /device:TPU:1, one launch (start us, length us, event | category | flops | bytes accessed | tf_op | source)
XLA Modules:
  0.0 940.7 jit_solution(14607773695680848863)
XLA Ops:
  7.9 2.0 copy.158
  9.9 10.2 %all-to-all-start = ((bf16[128,8,192]{0,2,1:T(8,128)(2,1)}), bf16[128,8,192]{0,2,1:T(8,128)(2,1)S(1)}, u32[]{:S(2)}, u32[]{:S(2)}) async-start(bf16[128,8,192]{0,2,1:T(8,128)(2,1)} %bitcast.31), calls=%async_computation | async-start | bytes 786432 | tf_op jit(solution)/shard_map/all_to_all | solution.py:89
  21.0 7.2 all-to-all-done
  28.2 4.2 all-to-all-start.1
  33.4 7.6 all-to-all-done.1
  41.0 4.1 all-to-all-start.2
  50.0 3.2 all-to-all-done.2
  55.9 31.0 %while.30 = (s32[]{:T(128)}, bf16[3,32,32,64]{3,2,1,0:T(8,128)(2,1)}, f32[3,32,32,1]{2,1,3,0:T(8,128)}, s32[3]{0:T(128)S(1)}, s32[3,32]{1,0:T(4,128)S(1)}, /*ind...) while((s32[]{:T(128)}, ...), condition=%wide.region_3.4_spmd, body=%wide.region_0.3_spmd.sunk | while | flops 51781700 | bytes 8198467 | solution.py:113
  61.6 2.1 fusion.118
  64.8 1.5 fusion.119
  72.0 2.1 fusion.118
  75.1 1.5 fusion.119
  82.3 2.1 fusion.118
  85.4 1.5 fusion.119
  86.9 1.8 copy.168
  91.0 70.4 %all-gather.5.cloned.1.call-done = bf16[24576,96]{1,0:T(8,128)(2,1)} async-done(((bf16[192,96]{1,0:T(8,128)(2,1)}), bf16[24576,96]{1,0:T(8,128)(2,1)}) %all-gather.5.cloned.1.call-update) | async-done | bytes 4718608 | tf_op jit(solution)/shard_map/all_gather | solution.py:117
  161.5 9.4 copy.172
  170.8 10.7 %dot_general.75 = bf16[1536,96,16]{0,1,2:T(8,128)(2,1)} reshape(bf16[8,192,96,16]{1,0,2,3:T(8,128)(2,1)} %bitcast.247) | data formatting | bytes 9437184 | tf_op jit(solution)/shard_map/tfc,sfrc->tsr/dot_general | solution.py:127
  181.5 3.3 fusion.71
  185.7 3.6 all-to-all-start.4
  189.3 4.7 all-gather.7.cloned.1.call-done
  194.0 4.4 fusion.68
  198.5 3.9 all-to-all-start.3
  205.0 89.6 %while.31 = (s32[]{:T(128)}, bf16[3,32,32,64]{3,2,1,0:T(8,128)(2,1)}, bf16[3,32,32,64]{3,1,2,0:T(8,128)(2,1)}, bf16[3,32,32,64]{3,1,2,0:T(8,128)(2,1)}, s32[3]{0...) while((s32[]{:T(128)}, ...), condition=%wide.region_6.7_spmd, body=%wide.region_4.6_spmd.sunk | while | flops 430145792 | bytes 28231952 | solution.py:148
  211.2 2.0 fusion.135
  213.3 2.0 gather_fusion.3
  216.5 2.6 fusion.137
  219.1 1.4 fusion.138
  220.5 2.8 convolution_multiply_fusion.5
  223.4 2.2 copy.238
  225.6 3.8 fusion.140
  229.4 1.6 fusion.141
  231.0 3.8 fusion.142
  241.1 2.0 fusion.135
  243.1 2.0 gather_fusion.3
  245.1 1.2 fusion.136
  246.4 2.6 fusion.137
  249.0 1.4 fusion.138
  250.4 2.8 convolution_multiply_fusion.5
  253.2 2.2 copy.238
  255.5 3.8 fusion.140
  259.3 1.6 fusion.141
  260.9 3.8 fusion.142
  270.9 2.0 fusion.135
  273.0 2.0 gather_fusion.3
  275.0 1.2 fusion.136
  276.2 2.6 fusion.137
  278.8 1.4 fusion.138
  280.3 2.8 convolution_multiply_fusion.5
  283.1 2.2 copy.238
  285.4 3.8 fusion.140
  289.2 1.6 fusion.141
  290.8 3.8 fusion.142
  294.6 1.8 copy.181
  298.0 4.8 all-to-all-start.5
  305.1 5.8 all-to-all-done.5
  310.9 4.2 all-to-all-start.6
  315.1 569.4 %reduce-scatter.2.cloned.1.call-done = f32[192,24]{0,1:T(8,128)} async-done(((f32[192,1536]{0,1:T(8,128)}), f32[192,24]{0,1:T(8,128)}) %reduce-scatter.2.cloned.1.call-update) | async-done | bytes 18448 | tf_op jit(solution)/shard_map/reduce_scatter | solution.py:157
  884.5 1.3 broadcast_multiply_fusion
  885.8 9.5 %copy.226 = bf16[8,16,192,96]{3,1,2,0:T(8,128)(2,1)} copy(bf16[8,16,192,96]{3,2,1,0:T(8,128)(2,1)} %bitcast.245) | data formatting | bytes 9437184 | tf_op jit(solution)/shard_map/reshape | solution.py:118
  895.3 11.3 %dot_general.72 = bf16[1536,192,8]{0,1,2:T(8,128)(2,1)} reshape(bf16[16,96,192,8]{1,0,2,3:T(8,128)(2,1)} %bitcast.246) | data formatting | bytes 9437184 | tf_op jit(solution)/shard_map/tsr,sfrc->tfc/dot_general | solution.py:121
  908.9 16.3 %all-to-all-start.7 = ((bf16[8,128,192]{1,2,0:T(8,128)(2,1)}), bf16[8,128,192]{1,2,0:T(8,128)(2,1)S(1)}, u32[]{:S(2)}, u32[]{:S(2)}) async-start(bf16[8,128,192]{1,2,0:T(8,128)(2,1)} %copy.186), calls=%async_computation.7 | async-start | bytes 786432 | tf_op jit(solution)/shard_map/all_to_all | solution.py:152
  925.2 3.9 fusion.72
  930.9 2.3 all-to-all-done.7
  (175 shorter events, 53.3 us)
Async XLA Ops:
  7.2 13.0 %copy-start.6 = (bf16[1,128,1536]{2,1,0:T(8,128)(2,1)S(1)}, bf16[1,128,1536]{2,1,0:T(8,128)(2,1)}, u32[]{:S(2)}) copy-start(bf16[1,128,1536]{2,1,0:T(8,128)(2,1)} %param.12) | copy-start | bytes 1179652
  7.2 154.3 %all-gather.5.cloned.1.call-start = ((), (), s32[]{:S(2)}) async-start(), calls=%async_computation.10 | async-start | bytes 6340608 | tf_op jit(solution)/shard_map/all_gather | solution.py:117
  7.9 24.5 %copy-start.7 = (bf16[1,128,1536]{2,1,0:T(8,128)(2,1)S(1)}, bf16[1,128,1536]{2,1,0:T(8,128)(2,1)}, u32[]{:S(2)}) copy-start(bf16[1,128,1536]{2,1,0:T(8,128)(2,1)} %param.13) | copy-start | bytes 1179652
  9.9 18.3 %all-to-all-start = ((bf16[128,8,192]{0,2,1:T(8,128)(2,1)}), bf16[128,8,192]{0,2,1:T(8,128)(2,1)S(1)}, u32[]{:S(2)}, u32[]{:S(2)}) async-start(bf16[128,8,192]{0,2,1:T(8,128)(2,1)} %bitcast.31), calls=%async_computation | async-start | bytes 786432 | tf_op jit(solution)/shard_map/all_to_all | solution.py:89
  21.0 24.8 %copy-start.2 = (bf16[1,128,1536]{2,1,0:T(8,128)(2,1)S(1)}, bf16[1,128,1536]{2,1,0:T(8,128)(2,1)}, u32[]{:S(2)}) copy-start(bf16[1,128,1536]{2,1,0:T(8,128)(2,1)} %param.14) | copy-start | bytes 1179652
  28.2 12.8 %all-to-all-start.1 = ((bf16[128,8,192]{0,2,1:T(8,128)(2,1)}), bf16[128,8,192]{0,2,1:T(8,128)(2,1)S(1)}, u32[]{:S(2)}, u32[]{:S(2)}) async-start(bf16[128,8,192]{0,2,1:T(8,128)(2,1)} %bitcast.33), calls=%async_computation.1 | async-start | bytes 786432 | tf_op jit(solution)/shard_map/all_to_all | solution.py:90
  32.4 14.3 %copy-start.10 = (s32[1,3,32]{2,0,1:T(1,128)S(1)}, s32[1,3,32]{2,0,1:T(1,128)}, u32[]{:S(2)}) copy-start(s32[1,3,32]{2,0,1:T(1,128)} %param.17) | copy-start | bytes 1156
  32.4 14.3 %copy-start.8 = (s32[1,3,32,6]{2,0,3,1:T(1,128)S(1)}, s32[1,3,32,6]{2,0,3,1:T(1,128)}, u32[]{:S(2)}) copy-start(s32[1,3,32,6]{2,0,3,1:T(1,128)} %param.16) | copy-start | bytes 6916
  41.0 12.2 %all-to-all-start.2 = ((bf16[128,8,192]{0,2,1:T(8,128)(2,1)}), bf16[128,8,192]{0,2,1:T(8,128)(2,1)S(1)}, u32[]{:S(2)}, u32[]{:S(2)}) async-start(bf16[128,8,192]{0,2,1:T(8,128)(2,1)} %bitcast.35), calls=%async_computation.2 | async-start | bytes 786432 | tf_op jit(solution)/shard_map/all_to_all | solution.py:91
  45.1 148.9 %all-gather.7.cloned.1.call-start = ((), (), s32[]{:S(2)}) async-start(), calls=%async_computation.11 | async-start | bytes 3538944 | tf_op jit(solution)/shard_map/all_gather | solution.py:125
  86.9 2.5 copy-start.9
  170.8 10.7 %copy-start.3 = (bf16[1,128,1536]{1,2,0:T(8,128)(2,1)S(1)}, bf16[1,128,1536]{1,2,0:T(8,128)(2,1)}, u32[]{:S(2)}) copy-start(bf16[1,128,1536]{1,2,0:T(8,128)(2,1)} %copy.171) | copy-start | bytes 1179652
  185.7 12.8 %all-to-all-start.4 = ((bf16[128,8,192]{0,2,1:T(8,128)(2,1)}), bf16[128,8,192]{0,2,1:T(8,128)(2,1)S(1)}, u32[]{:S(2)}, u32[]{:S(2)}) async-start(bf16[128,8,192]{0,2,1:T(8,128)(2,1)} %bitcast.46), calls=%async_computation.4 | async-start | bytes 786432 | tf_op jit(solution)/shard_map/all_to_all | solution.py:133
  189.3 695.2 %reduce-scatter.2.cloned.1.call-start = ((), (), s32[]{:S(2)}) async-start(), calls=%async_computation.9 | async-start | bytes 1597440 | tf_op jit(solution)/shard_map/reduce_scatter | solution.py:157
  198.5 99.6 %all-to-all-start.3 = ((bf16[8,128,192]{1,2,0:T(8,128)(2,1)}), bf16[8,128,192]{1,2,0:T(8,128)(2,1)S(1)}, u32[]{:S(2)}, u32[]{:S(2)}) async-start(bf16[8,128,192]{1,2,0:T(8,128)(2,1)} %copy.169), calls=%async_computation.3 | async-start | bytes 786432 | tf_op jit(solution)/shard_map/all_to_all | solution.py:115
  205.0 2.5 copy-start.11
  213.2 3.3 copy-start
  225.6 3.8 copy-start.1
  231.0 3.8 copy-start.12
  234.8 2.5 copy-start.11
  243.1 3.3 copy-start
  255.5 3.8 copy-start.1
  260.9 3.8 copy-start.12
  264.7 2.5 copy-start.11
  273.0 3.3 copy-start
  285.4 3.8 copy-start.1
  290.8 3.8 copy-start.12
  296.4 6.4 copy-start.4
  298.0 12.9 %all-to-all-start.5 = ((bf16[8,128,192]{1,2,0:T(8,128)(2,1)}), bf16[8,128,192]{1,2,0:T(8,128)(2,1)S(1)}, u32[]{:S(2)}, u32[]{:S(2)}) async-start(bf16[8,128,192]{1,2,0:T(8,128)(2,1)} %copy.182), calls=%async_computation.5 | async-start | bytes 786432 | tf_op jit(solution)/shard_map/all_to_all | solution.py:150
  310.9 598.0 %all-to-all-start.6 = ((bf16[8,128,192]{1,2,0:T(8,128)(2,1)}), bf16[8,128,192]{1,2,0:T(8,128)(2,1)S(1)}, u32[]{:S(2)}, u32[]{:S(2)}) async-start(bf16[8,128,192]{1,2,0:T(8,128)(2,1)} %copy.184), calls=%async_computation.6 | async-start | bytes 786432 | tf_op jit(solution)/shard_map/all_to_all | solution.py:151
  895.3 11.3 %copy-start.5 = (bf16[3,32,32,64]{3,1,2,0:T(8,128)(2,1)S(1)}, bf16[3,32,32,64]{3,1,2,0:T(8,128)(2,1)}, u32[]{:S(2)}) copy-start(bf16[3,32,32,64]{3,1,2,0:T(8,128)(2,1)} %get-tuple-element.288) | copy-start | bytes 1179652
  908.9 24.3 %all-to-all-start.7 = ((bf16[8,128,192]{1,2,0:T(8,128)(2,1)}), bf16[8,128,192]{1,2,0:T(8,128)(2,1)S(1)}, u32[]{:S(2)}, u32[]{:S(2)}) async-start(bf16[8,128,192]{1,2,0:T(8,128)(2,1)} %copy.186), calls=%async_computation.7 | async-start | bytes 786432 | tf_op jit(solution)/shard_map/all_to_all | solution.py:152
Sparse Core Ops, SparseCore 0:
  11.1 150.2 all-gather.4
  163.6 30.3 all-gather.6
  198.6 685.8 reduce-scatter.1
where the time goes:
time: 944 us; the launch traced here: 941 us
  waiting for transfers between devices  672 us (71%)
  local copies, waits for them, and re-layouts  106 us (11%)
  matrix products  76.4 us (8%)
  starting transfers between devices  51.3 us (5%)
  between operations  14 us (1%)
  loops' own time  12.2 us (1%)
    reduce_scatter x1, waiting for transfers between devices, per_device(): lax.psum_scatter(weight_term, ('fsdp', 'dp'), scatter_dimension=1, tiled=...  569 us
    all_gather x1, waiting for transfers between devices, per_device(): lax.all_gather(out_weight[None], ('seq', 'fsdp'), axis=0, tiled=True)  70.4 us
  transfers between devices with their start and end apart: 11, of which 8 were waited for; matrix products, arithmetic and copies ran while one was open for 20% of the time, Pallas kernels for 0%

commit v1 on v0

v1 whole, which is shorter than its diff:
```python
import functools

import jax
import jax.numpy as jnp
from jax import lax
from jax.experimental import pallas as pl
from jax.experimental.pallas import tpu as pltpu
from jax.sharding import Mesh
from jax.sharding import PartitionSpec as P

BF16 = jnp.bfloat16
F32 = jnp.float32
HEAD_DIM = 64
FRAME = 64
SCORE_SCALE = HEAD_DIM ** (-0.5)
LOG2_E = 1.4426950408889634
DROPPED = -1e30
NT = (((1,), (1,)), ((), ()))
NN = (((1,), (0,)), ((), ()))


def dot(left, right, dims):
    return lax.dot_general(left, right, dims, preferred_element_type=F32)


def call(kernel, out_shape, operands, in_specs=None, scratch=()):
    vmem = pl.BlockSpec(memory_space=pltpu.VMEM)
    return pl.pallas_call(
        kernel,
        out_shape=out_shape,
        in_specs=in_specs or [vmem] * len(operands),
        out_specs=jax.tree.map(lambda _: vmem, out_shape),
        scratch_shapes=list(scratch),
        compiler_params=pltpu.CompilerParams(vmem_limit_bytes=56 * 2**20),
    )(*operands)


def pack_kernel(query_ref, key_ref, value_ref, out_ref):
    peers = out_ref.shape[0]
    width = query_ref.shape[1] // peers
    for place, ref in enumerate((query_ref, key_ref, value_ref)):
        turned = ref[...].T
        for peer in range(peers):
            out_ref[peer, place * width : (place + 1) * width, :] = turned[
                peer * width : (peer + 1) * width
            ]


def unpack_kernel(x_ref, *out_refs):
    peers = x_ref.shape[0]
    width = x_ref.shape[1] // len(out_refs)
    for place, ref in enumerate(out_refs):
        stacked = jnp.concatenate(
            [x_ref[peer, place * width : (place + 1) * width, :] for peer in range(peers)], axis=0
        )
        ref[...] = stacked.T


def join_columns_kernel(x_ref, out_ref):
    width = x_ref.shape[2]
    for place in range(x_ref.shape[0]):
        out_ref[:, place * width : (place + 1) * width] = x_ref[place]


def window_start(block, blocks, block_frames, window_frames):
    return min(max(block * block_frames - 1, 0), blocks * block_frames - window_frames)


def keep_bias(shift, keys, queries, count):
    key_at = lax.broadcasted_iota(jnp.int32, (keys, queries), 0)
    query_at = lax.broadcasted_iota(jnp.int32, (keys, queries), 1)
    frames_off = jnp.abs(key_at // FRAME + shift - query_at // FRAME)
    same_row = (key_at // 32) % 2 == (query_at // 32) % 2
    frame_reach = jnp.where(count >= 3, 1, 0)
    row_reach = jnp.where(count % 2 == 0, 1, 0)
    rows_off = jnp.where(same_row, 0, 1)
    return jnp.where((frames_off <= frame_reach) & (rows_off <= row_reach), 0.0, DROPPED)


def plan(x_ref):
    blocks, _, block_tokens = x_ref.shape
    block_frames = block_tokens // FRAME
    return blocks, block_tokens, block_frames, block_frames + 2


def rows_of(x_ref, part, head, local_heads):
    at = (part * local_heads + head) * HEAD_DIM
    return jnp.concatenate(
        [x_ref[block, at : at + HEAD_DIM, :] for block in range(x_ref.shape[0])], axis=1
    )


def forward_kernel(count_ref, x_ref, attended_ref, log_ref):
    local_heads = count_ref.shape[0]
    blocks, block_tokens, block_frames, window_frames = plan(x_ref)
    window = window_frames * FRAME
    for head in range(local_heads):
        count = count_ref[head, 2]
        query_t = rows_of(x_ref, 0, head, local_heads)
        key_rows = rows_of(x_ref, 1, head, local_heads).T
        value_t = rows_of(x_ref, 2, head, local_heads)
        biases = {}
        for block in range(blocks):
            first = window_start(block, blocks, block_frames, window_frames)
            shift = first - block * block_frames
            if shift not in biases:
                biases[shift] = keep_bias(shift, window, block_tokens, count)
            here = slice(block * block_tokens, (block + 1) * block_tokens)
            near = slice(first * FRAME, first * FRAME + window)
            scores = (
                dot(key_rows[near], query_t[:, here], NN) * (SCORE_SCALE * LOG2_E) + biases[shift]
            )
            top = jnp.max(scores, axis=0, keepdims=True)
            raw = jnp.exp2(scores - top)
            total = jnp.sum(raw, axis=0, keepdims=True)
            rounded = (raw * (1.0 / total)).astype(BF16)
            attended_ref[block, head * HEAD_DIM : (head + 1) * HEAD_DIM, :] = dot(
                value_t[:, near], rounded, NN
            ).astype(BF16)
            log_ref[head, :, here] = top + jnp.log2(total)


def backward_kernel(count_ref, x_ref, attended_ref, log_ref, up_ref, out_ref, key_sum, value_sum):
    local_heads = count_ref.shape[0]
    blocks, block_tokens, block_frames, window_frames = plan(x_ref)
    window = window_frames * FRAME
    for head in range(local_heads):
        count = count_ref[head, 2]
        query_t = rows_of(x_ref, 0, head, local_heads)
        key_t = rows_of(x_ref, 1, head, local_heads)
        key_rows = key_t.T
        value_rows = rows_of(x_ref, 2, head, local_heads).T
        at = slice(head * HEAD_DIM, (head + 1) * HEAD_DIM)
        key_sum[...] = jnp.zeros_like(key_sum)
        value_sum[...] = jnp.zeros_like(value_sum)
        biases = {}
        for block in range(blocks):
            first = window_start(block, blocks, block_frames, window_frames)
            shift = first - block * block_frames
            if shift not in biases:
                biases[shift] = keep_bias(shift, window, block_tokens, count)
            here = slice(block * block_tokens, (block + 1) * block_tokens)
            near = slice(first * FRAME, first * FRAME + window)
            query_here = query_t[:, here]
            up_here = up_ref[at, here]
            scores = dot(key_rows[near], query_here, NN) * (SCORE_SCALE * LOG2_E) + biases[shift]
            weights = jnp.exp2(scores - log_ref[head, :, here])
            inner = jnp.sum(
                up_here.astype(F32) * attended_ref[block, at, :].astype(F32), axis=0, keepdims=True
            )
            prob_grad = dot(value_rows[near], up_here, NN)
            score_grad = (weights * (prob_grad - inner)).astype(BF16)
            rounded = weights.astype(BF16)
            out_ref[block, at, :] = (dot(key_t[:, near], score_grad, NN) * SCORE_SCALE).astype(BF16)
            key_sum[near, :] += dot(score_grad, query_here, NT)
            value_sum[near, :] += dot(rounded, up_here, NT)
        key_grad = (key_sum[...] * SCORE_SCALE).T.astype(BF16)
        value_grad = value_sum[...].T.astype(BF16)
        for block in range(blocks):
            here = slice(block * block_tokens, (block + 1) * block_tokens)
            for part, grad in ((1, key_grad), (2, value_grad)):
                row = (part * local_heads + head) * HEAD_DIM
                out_ref[block, row : row + HEAD_DIM, :] = grad[:, here]


def joined(ref):
    return jnp.concatenate([ref[block] for block in range(ref.shape[0])], axis=1)


def weight_kernel(attended_ref, grad_ref, out_ref, *, column_parts):
    term = dot(joined(attended_ref), grad_ref[...], NN).T
    dp_size = out_ref.shape[0]
    wide = out_ref.shape[1] // column_parts
    for peer in range(dp_size):
        out_ref[peer] = jnp.concatenate(
            [
                term[(part * dp_size + peer) * wide : (part * dp_size + peer + 1) * wide]
                for part in range(column_parts)
            ],
            axis=0,
        ).astype(BF16)


def upstream_kernel(weight_ref, grad_ref, out_ref):
    out_ref[...] = dot(weight_ref[...], grad_ref[...], NT).astype(BF16)


def layer_kernel(attended_ref, weight_ref, out_ref):
    peers, width, tokens = attended_ref.shape
    rows = attended_ref[...].reshape(peers * width, tokens).T
    out_ref[...] = dot(rows, weight_ref[...], NN).astype(BF16)


def per_device(query_in, key_in, value_in, out_grad, out_weight, key_tiles, key_count):
    seq_size = lax.axis_size("seq")
    fsdp_size = lax.axis_size("fh") * lax.axis_size("fl")
    dp_size = lax.axis_size("dp")
    _, local_tokens, model = query_in.shape
    all_tokens = local_tokens * seq_size
    width = model // seq_size
    local_heads = width // HEAD_DIM
    counts = key_count[0]
    smem = pl.BlockSpec(memory_space=pltpu.SMEM)
    vmem = pl.BlockSpec(memory_space=pltpu.VMEM)
    shape = jax.ShapeDtypeStruct

    grad_all = lax.all_gather(out_grad[0], "seq", axis=0, tiled=True)
    packed = call(
        pack_kernel,
        shape((seq_size, 3 * width, local_tokens), BF16),
        (query_in[0], key_in[0], value_in[0]),
    )
    heads = lax.all_to_all(packed, "seq", split_axis=0, concat_axis=0, tiled=True)
    near_weight = lax.all_gather(out_weight, "fl", axis=0, tiled=False)
    row_weight = lax.all_gather(near_weight, "fh", axis=0, tiled=True)
    row_weight = call(join_columns_kernel, shape((width, model), BF16), (row_weight,))
    full_weight = lax.all_gather(row_weight, "seq", axis=0, tiled=True)

    attended, log_total = call(
        forward_kernel,
        (
            shape((seq_size, width, local_tokens), BF16),
            shape((local_heads, 1, all_tokens), F32),
        ),
        (counts, heads),
        in_specs=[smem, vmem],
    )
    attended_tokens = lax.all_to_all(attended, "seq", split_axis=0, concat_axis=0, tiled=True)

    columns = model // (fsdp_size * dp_size)
    term = call(
        functools.partial(weight_kernel, column_parts=fsdp_size),
        shape((dp_size, fsdp_size * columns, width), BF16),
        (attended, grad_all),
    )
    term = lax.all_to_all(term, "dp", split_axis=0, concat_axis=0, tiled=True)
    term = jnp.sum(term.astype(F32), axis=0).astype(BF16)
    term = term.reshape(fsdp_size, columns, width)
    term = lax.all_to_all(term, ("fh", "fl"), split_axis=0, concat_axis=0, tiled=True)
    weight_grad = jnp.sum(term.astype(F32), axis=0).T / (fsdp_size * dp_size)

    upstream = call(upstream_kernel, shape((width, all_tokens), BF16), (row_weight, grad_all))
    grads = call(
        backward_kernel,
        shape((seq_size, 3 * width, local_tokens), BF16),
        (counts, heads, attended, log_total, upstream),
        in_specs=[smem] + [vmem] * 4,
        scratch=[pltpu.VMEM((all_tokens, HEAD_DIM), F32)] * 2,
    )
    grads = lax.all_to_all(grads, "seq", split_axis=0, concat_axis=0, tiled=True)
    query_grad, key_grad, value_grad = call(
        unpack_kernel, (shape((local_tokens, model), BF16),) * 3, (grads,)
    )
    layer_out = call(
        layer_kernel, shape((local_tokens, model), BF16), (attended_tokens, full_weight)
    )
    return (layer_out[None], query_grad[None], key_grad[None], value_grad[None], weight_grad)


def solution(mesh):
    seq_size, fsdp_size, dp_size = (mesh.shape[name] for name in ("seq", "fsdp", "dp"))
    order = [mesh.axis_names.index(name) for name in ("seq", "fsdp", "dp")]
    devices = mesh.devices.transpose(order).reshape(seq_size, fsdp_size // 4, 4, dp_size)
    split_mesh = Mesh(devices, ("seq", "fh", "fl", "dp"))
    clips = ("fh", "fl", "dp")
    tokens = P(clips, "seq", None)
    return jax.shard_map(
        per_device,
        mesh=split_mesh,
        in_specs=(
            tokens,
            tokens,
            tokens,
            tokens,
            P("seq", ("fh", "fl")),
            P(clips, "seq", None, None),
            P(clips, "seq", None),
        ),
        out_specs=(tokens, tokens, tokens, tokens, P("seq", clips)),
        check_vma=False,
    )
```

time: 944 us -> 191 us (0.20)
  waiting for transfers between devices: 672 us -> 24.4 us
  local copies, waits for them, and re-layouts: 106 us -> 4.71 us
  blocking collectives: 0 us -> 86.7 us
  matrix products: 76.4 us -> 0 us
  Pallas kernels: 0 us -> 35.7 us
  starting transfers between devices: 51.3 us -> 24.3 us
  loops' own time: 12.2 us -> 0 us
    reduce_scatter x1 -> x0, waiting for transfers between devices: 569 us -> none  [per_device(): lax.psum_scatter(weight_term, ('fsdp', 'dp'), scatter_dimension=1, tiled=...]
    dot_general x30 -> x0, matrix products: 76.4 us -> none  [the longest x3 11.4 us: head_backward(): jnp.einsum('nst,nsrd->trd', one_hot, key_slots.reshape(slot_shape), preci...]
    all_gather x1, waiting for transfers between devices: 70.4 us -> 0.01 us  [per_device(): full_weight = lax.all_gather(row_weight, 'seq', axis=0, tiled=True)]
    all_gather x0 -> x2, blocking collectives: none -> 47.2 us  [the longest x1 33.6 us: per_device(): row_weight = lax.all_gather(near_weight, 'fh', axis=0, tiled=True)]
    all_to_all x0 -> x2, blocking collectives: none -> 39.5 us  [the longest x1 27.6 us: per_device(): lax.all_to_all(grads, 'seq', split_axis=0, concat_axis=0, tiled=True)]
    pallas_call x0 -> x8, Pallas kernels: none -> 35.7 us  [call(): pl.pallas_call(kernel, out_shape=out_shape, in_specs=in_specs or [vmem] *...]
    all_to_all x8 -> x3, starting transfers between devices: 51.3 us -> 24.2 us  [the longest x1 10.5 us: per_device(): lax.all_to_all(packed, 'seq', split_axis=0, concat_axis=0, tiled=True)]
    dot_general x2 -> x0, local copies, waits for them, and re-layouts: 21.9 us -> none  [the longest x1 11.3 us: per_device(): jnp.einsum('tsr,' + weight_code + '->tfc', attn_split, full_weight, prefe...]
  transfers between devices with their start and end apart: 11 -> 5, of which waited for: 8 -> 3; matrix products, arithmetic and copies ran while one was open for 20% -> 2% of each run, Pallas kernels for 0% -> 17%
where the time goes in v1:
time: 191 us
  blocking collectives  86.7 us (45%)
  Pallas kernels  35.7 us (19%)
  waiting for transfers between devices  24.4 us (13%)
  starting transfers between devices  24.3 us (13%)
  between operations  14.1 us (7%)
  local copies, waits for them, and re-layouts  4.71 us (2%)
    pallas_call x8, Pallas kernels, call(): pl.pallas_call(kernel, out_shape=out_shape, in_specs=in_specs or [vmem] *...  35.7 us
    all_gather x1, blocking collectives, per_device(): row_weight = lax.all_gather(near_weight, 'fh', axis=0, tiled=True)  33.6 us
    all_to_all x1, blocking collectives, per_device(): lax.all_to_all(grads, 'seq', split_axis=0, concat_axis=0, tiled=True)  27.6 us
    all_to_all x1, waiting for transfers between devices, per_device(): lax.all_to_all(packed, 'seq', split_axis=0, concat_axis=0, tiled=True)  18.7 us
    all_gather x1, blocking collectives, per_device(): near_weight = lax.all_gather(out_weight, 'fl', axis=0, tiled=False)  13.6 us
    all_to_all x1, blocking collectives, per_device(): term = lax.all_to_all(term, 'dp', split_axis=0, concat_axis=0, tiled=True)  11.9 us
    all_to_all x1, starting transfers between devices, per_device(): lax.all_to_all(packed, 'seq', split_axis=0, concat_axis=0, tiled=True)  10.5 us
    all_to_all x1, starting transfers between devices, per_device(): lax.all_to_all(term, ('fh', 'fl'), split_axis=0, concat_axis=0, tiled=True)  9.42 us
  transfers between devices with their start and end apart: 5, of which 3 were waited for; matrix products, arithmetic and copies ran while one was open for 2% of the time, Pallas kernels for 17%

profile of v1, /device:TPU:1, one launch (start us, length us, event | category | flops | bytes accessed | tf_op | source)
XLA Modules:
  0.0 190.5 jit_solution(2208764225166860170)
XLA Ops:
  7.2 0.0 all-gather.7.cloned.1.call-start
  7.2 0.7 all-gather.7.cloned.1.call-update
  7.9 0.0 all-gather.5.cloned.1.call-start
  7.9 13.6 %all-gather = bf16[768,96]{1,0:T(8,128)(2,1)S(1)} all-gather(bf16[192,96]{1,0:T(8,128)(2,1)} %param.11), channel_id=2, replica_groups=mesh['seq'=8,'fh'=4,'fl'=4,'dp'=4] {'fl'}, dimensions={0}, use_global_device_ids=true | all-gather | bytes 184320 | tf_op jit(solution)/shard_map/all_gather | solution.py:214
  21.6 33.6 %all_gather.17.x_ref = bf16[16,192,96]{2,1,0:T(8,128)(2,1)} all-gather(bf16[4,192,96]{2,1,0:T(8,128)(2,1)S(1)} %bitcast.17), channel_id=1, replica_groups=mesh['seq'=8,'fh'=4,'fl'=4,'dp'=4] {'fh'}, dimensions={0}, use_global_device_ids=true | all-gather | bytes 737280 | tf_op jit(solution)/shard_map/all_gather | solution.py:215
  55.1 2.3 %shard_map.103.weight_ref = bf16[192,1536]{1,0:T(8,128)(2,1)} custom-call(bf16[16,192,96]{2,1,0:T(8,128)(2,1)} %all_gather.17.x_ref), custom_call_target="tpu_custom_call" | custom-call | tf_op jit(solution)/shard_map/pallas_call | solution.py:28
  57.4 0.0 all-gather.5.cloned.1.call-update
  57.4 2.7 %shard_map.101 = bf16[8,576,128]{2,1,0:T(8,128)(2,1)} custom-call(bf16[128,1536]{1,0:T(8,128)(2,1)} %bitcast.18, bf16[128,1536]{1,0:T(8,128)(2,1)} %bitcast.19, bf16[128,1536]{1,0:T(8,128)(2,1)} %bitcast.20), custom_call_target="tpu_custom_call" | custom-call | tf_op jit(solution)/shard_map/pallas_call | solution.py:28
  60.1 0.0 copy-start.2
  60.1 10.5 %all-to-all-start = ((bf16[8,576,128]{2,1,0:T(8,128)(2,1)}), bf16[8,576,128]{2,1,0:T(8,128)(2,1)S(1)}, u32[]{:S(2)}, u32[]{:S(2)}) async-start(bf16[8,576,128]{2,1,0:T(8,128)(2,1)} %shard_map.101), calls=%async_computation | async-start | bytes 2359296 | tf_op jit(solution)/shard_map/all_to_all | solution.py:213
  70.7 0.0 copy-done.2
  70.7 0.6 copy.17
  71.2 18.7 %all-to-all-done.x_ref = bf16[8,576,128]{2,1,0:T(8,128)(2,1)S(1)} async-done(((bf16[8,576,128]{2,1,0:T(8,128)(2,1)}), bf16[8,576,128]{2,1,0:T(8,128)(2,1)S(1)}, u32[]{:S(2)}, u32[]{:S(2)}) %all-to-all-start) | async-done | bytes 1179680 | tf_op jit(solution)/shard_map/all_to_all | solution.py:213
  89.9 0.0 copy-start
  89.9 1.1 copy-done
  91.0 8.1 %shard_map.102 = (bf16[8,192,128]{2,1,0:T(8,128)(2,1)}, f32[3,1,1024]{2,1,0:T(1,128)}) custom-call(s32[3,32]{1,0:T(4,128)} %bitcast.22, bf16[8,576,128]{2,1,0:T(8,128)(2,1)} %copy-done), custom_call_target="tpu_custom_call" | custom-call | tf_op jit(solution)/shard_map/pallas_call | solution.py:28
  99.1 0.0 all-gather.7.cloned.1.call-done
  99.1 3.9 %shard_map.108 = bf16[4,384,192]{2,1,0:T(8,128)(2,1)} custom-call(bf16[8,192,128]{2,1,0:T(8,128)(2,1)} %get-tuple-element.10.attended_ref, bf16[1024,1536]{1,0:T(8,128)(2,1)} %bitcast.15), custom_call_target="tpu_custom_call" | custom-call | tf_op jit(solution)/shard_map/pallas_call | solution.py:28
  103.0 1.5 copy.13
  104.4 11.9 %all_to_all.25 = bf16[4,384,192]{1,2,0:T(8,128)(2,1)S(1)} all-to-all(bf16[4,384,192]{1,2,0:T(8,128)(2,1)S(1)} %copy.13), channel_id=1, replica_groups=mesh['seq'=8,'fh'=4,'fl'=4,'dp'=4] {'dp'}, dimensions={0} | all-to-all | bytes 1179648 | tf_op jit(solution)/shard_map/all_to_all | solution.py:236
  116.4 0.1 reduce_sum.21
  116.5 0.8 copy.14
  117.3 9.4 %all-to-all-start.4 = ((bf16[16,24,192]{2,1,0:T(8,128)(2,1)}), bf16[16,24,192]{2,1,0:T(8,128)(2,1)S(1)}, u32[]{:S(2)}, u32[]{:S(2)}) async-start(bf16[16,24,192]{2,1,0:T(8,128)(2,1)} %bitcast.9), calls=%async_computation.4 | async-start | bytes 393216 | tf_op jit(solution)/shard_map/all_to_all | solution.py:239
  126.7 4.0 %shard_map.105.up_ref = bf16[192,1024]{1,0:T(8,128)(2,1)} custom-call(bf16[192,1536]{1,0:T(8,128)(2,1)} %shard_map.103.weight_ref, bf16[1024,1536]{1,0:T(8,128)(2,1)} %bitcast.16), custom_call_target="tpu_custom_call" | custom-call | tf_op jit(solution)/shard_map/pallas_call | solution.py:28
  130.7 8.2 %shard_map.106 = bf16[8,576,128]{2,1,0:T(8,128)(2,1)} custom-call(s32[3,32]{1,0:T(4,128)} %bitcast.23, bf16[8,576,128]{2,1,0:T(8,128)(2,1)} %copy-done, bf16[8,192,128]{2,1,0:T(8,128)(2,1)} %get-tuple-element.10.attended_ref, f32[3,1,1024]{2,1,0:T(1,128)} %get-tuple-element.11.log_ref, bf16[192,1024]{1,0:T(8,128)(2,1)} %shard_map.105.up_ref), custom_call_target="tpu_custom_call" | custom-call | tf_op jit(solution)/shard_map/pallas_call | solution.py:28
  138.9 0.1 all-to-all-done.4
  139.0 27.6 %all_to_all.26.x_ref = bf16[8,576,128]{2,1,0:T(8,128)(2,1)} all-to-all(bf16[8,576,128]{2,1,0:T(8,128)(2,1)} %shard_map.106), channel_id=1, replica_groups=mesh['seq'=8,'fh'=4,'fl'=4,'dp'=4] {'seq'}, dimensions={0} | all-to-all | bytes 2359296 | tf_op jit(solution)/shard_map/all_to_all | solution.py:250
  166.6 4.2 %all-to-all-start.1 = ((bf16[8,192,128]{2,1,0:T(8,128)(2,1)}), bf16[8,192,128]{2,1,0:T(8,128)(2,1)S(1)}, u32[]{:S(2)}, u32[]{:S(2)}) async-start(bf16[8,192,128]{2,1,0:T(8,128)(2,1)} %get-tuple-element.10.attended_ref), calls=%async_computation.1 | async-start | bytes 786432 | tf_op jit(solution)/shard_map/all_to_all | solution.py:228
  170.8 0.6 multiply_bitcast_fusion
  171.5 2.4 %shard_map.107 = (bf16[128,1536]{1,0:T(8,128)(2,1)}, bf16[128,1536]{1,0:T(8,128)(2,1)}, bf16[128,1536]{1,0:T(8,128)(2,1)}) custom-call(bf16[8,576,128]{2,1,0:T(8,128)(2,1)} %all_to_all.26.x_ref), custom_call_target="tpu_custom_call" | custom-call | tf_op jit(solution)/shard_map/pallas_call | solution.py:28
  173.9 5.0 %all-to-all-done.1.attended_ref = bf16[8,192,128]{2,1,0:T(8,128)(2,1)S(1)} async-done(((bf16[8,192,128]{2,1,0:T(8,128)(2,1)}), bf16[8,192,128]{2,1,0:T(8,128)(2,1)S(1)}, u32[]{:S(2)}, u32[]{:S(2)}) %all-to-all-start.1) | async-done | bytes 393248 | tf_op jit(solution)/shard_map/all_to_all | solution.py:228
  178.9 0.0 copy-start.1
  178.9 0.0 all-gather.5.cloned.1.call-done.weight_ref
  178.9 0.8 copy-done.1
  179.7 4.0 %shard_map.104 = bf16[128,1536]{1,0:T(8,128)(2,1)} custom-call(bf16[8,192,128]{2,1,0:T(8,128)(2,1)} %copy-done.1, bf16[1536,1536]{1,0:T(8,128)(2,1)} %all-gather.5.cloned.1.call-done.weight_ref), custom_call_target="tpu_custom_call" | custom-call | tf_op jit(solution)/shard_map/pallas_call | solution.py:28
  (1 shorter events, 0.0 us)
Async XLA Ops:
  7.2 91.9 %all-gather.7.cloned.1.call-start = ((), (), s32[]{:S(2)}) async-start(), calls=%async_computation.6 | async-start | bytes 3538944 | tf_op jit(solution)/shard_map/all_gather | solution.py:207
  7.9 171.0 %all-gather.5.cloned.1.call-start = ((), (), s32[]{:S(2)}) async-start(), calls=%async_computation.5 | async-start | bytes 5308416 | tf_op jit(solution)/shard_map/all_gather | solution.py:217
  60.1 10.5 %copy-start.2 = (s32[1,3,32]{2,0,1:T(1,128)S(1)}, s32[1,3,32]{2,0,1:T(1,128)}, u32[]{:S(2)}) copy-start(s32[1,3,32]{2,0,1:T(1,128)} %param.12) | copy-start | bytes 1156
  60.1 29.8 %all-to-all-start = ((bf16[8,576,128]{2,1,0:T(8,128)(2,1)}), bf16[8,576,128]{2,1,0:T(8,128)(2,1)S(1)}, u32[]{:S(2)}, u32[]{:S(2)}) async-start(bf16[8,576,128]{2,1,0:T(8,128)(2,1)} %shard_map.101), calls=%async_computation | async-start | bytes 2359296 | tf_op jit(solution)/shard_map/all_to_all | solution.py:213
  89.9 1.1 copy-start
  117.3 21.7 %all-to-all-start.4 = ((bf16[16,24,192]{2,1,0:T(8,128)(2,1)}), bf16[16,24,192]{2,1,0:T(8,128)(2,1)S(1)}, u32[]{:S(2)}, u32[]{:S(2)}) async-start(bf16[16,24,192]{2,1,0:T(8,128)(2,1)} %bitcast.9), calls=%async_computation.4 | async-start | bytes 393216 | tf_op jit(solution)/shard_map/all_to_all | solution.py:239
  166.6 12.3 %all-to-all-start.1 = ((bf16[8,192,128]{2,1,0:T(8,128)(2,1)}), bf16[8,192,128]{2,1,0:T(8,128)(2,1)S(1)}, u32[]{:S(2)}, u32[]{:S(2)}) async-start(bf16[8,192,128]{2,1,0:T(8,128)(2,1)} %get-tuple-element.10.attended_ref), calls=%async_computation.1 | async-start | bytes 786432 | tf_op jit(solution)/shard_map/all_to_all | solution.py:228
  178.9 0.8 copy-start.1
Sparse Core Ops, SparseCore 0:
  10.1 41.1 all-gather.6
  57.6 50.8 all-gather.4

commit v2 on v1

v2 whole, which is shorter than its diff:
```python
import functools

import jax
import jax.numpy as jnp
from jax import lax
from jax.experimental import pallas as pl
from jax.experimental.pallas import tpu as pltpu
from jax.sharding import PartitionSpec as P

BF16 = jnp.bfloat16
F32 = jnp.float32
HEAD_DIM = 64
PAIR = 2 * HEAD_DIM
TILE = 32
FRAME = 64
FRAMES = 16
SCORE_SCALE = HEAD_DIM ** (-0.5)
LOG2_E = 1.4426950408889634
DROPPED = -1e30
NT = (((1,), (1,)), ((), ()))
NN = (((1,), (0,)), ((), ()))


def dot(left, right, dims):
    return lax.dot_general(left, right, dims, preferred_element_type=F32)


def call(kernel, out_shape, operands, scalars=0, us=2, after=()):
    vmem = pl.BlockSpec(memory_space=pltpu.VMEM)
    smem = pl.BlockSpec(memory_space=pltpu.SMEM)
    late = len(after)

    def body(*refs):
        kernel(*refs[late:])

    return pl.pallas_call(
        body,
        out_shape=out_shape,
        in_specs=[pl.BlockSpec(memory_space=pl.ANY)] * late
        + [smem] * scalars
        + [vmem] * (len(operands) - scalars),
        out_specs=jax.tree.map(lambda _: vmem, out_shape),
        cost_estimate=pl.CostEstimate(
            flops=int(us * 1e9), bytes_accessed=int(us * 3e6), transcendentals=0
        ),
        compiler_params=pltpu.CompilerParams(vmem_limit_bytes=56 * 2**20),
    )(*after, *operands)


def spread_weight_kernel(weight_ref, count_ref, out_ref, count_out_ref):
    rows, width = weight_ref.shape
    high = rows * width // 128
    piece = 128 - width
    pieces = [weight_ref[high:, at : at + piece] for at in range(0, width, piece)]
    dense = jnp.concatenate([weight_ref[:high, :], jnp.concatenate(pieces, axis=0)], axis=1)
    for peer in range(out_ref.shape[0]):
        out_ref[peer] = dense
    count_out_ref[...] = count_ref[...]


def join_weight_kernel(x_ref, out_ref):
    peers, high, _ = x_ref.shape
    width = out_ref.shape[1] // peers
    piece = 128 - width
    low = out_ref.shape[0] - high
    for peer in range(peers):
        out_ref[:high, peer * width : (peer + 1) * width] = x_ref[peer, :, :width]
        for at in range(width // piece):
            lane = peer * width + at * piece
            out_ref[high:, lane : lane + piece] = x_ref[peer, at * low : (at + 1) * low, width:]


def distances(place, keys, queries):
    key_at = lax.broadcasted_iota(jnp.int32, (keys, 2 * queries), 0)
    query_at = lax.broadcasted_iota(jnp.int32, (keys, 2 * queries), 1) % queries
    key_frame = key_at // FRAME - 1
    frames_off = jnp.abs(key_frame - query_at // FRAME)
    real_frame = key_frame + place * (queries // FRAME)
    frames_off = jnp.where((real_frame >= 0) & (real_frame < FRAMES), frames_off, FRAMES)
    rows_off = jnp.abs((key_at // TILE) % 2 - (query_at // TILE) % 2)
    return frames_off, rows_off


def by_head(first, second, queries):
    at = lax.broadcasted_iota(jnp.int32, (1, 2 * queries), 1)
    return jnp.where(at < queries, first, second)


def masked(scores, gaps, count_ref, pair, queries):
    counts = [count_ref[2 * pair + head, 2] for head in range(2)]
    frame_reach = by_head(*[jnp.where(count >= 3, 1, 0) for count in counts], queries)
    row_reach = by_head(*[jnp.where(count % 2 == 0, 1, 0) for count in counts], queries)
    kept = (gaps[0] <= frame_reach) & (gaps[1] <= row_reach)
    return jnp.where(kept, scores * (SCORE_SCALE * LOG2_E), DROPPED)


def window(left_ref, own_ref, right_ref, part, lanes):
    return jnp.concatenate(
        [left_ref[part, :, lanes], own_ref[:, lanes], right_ref[part, :, lanes]], axis=0
    )


def spread(pair, axis):
    at = lax.broadcasted_iota(jnp.int32, pair.shape, 1 - axis)
    zero = jnp.zeros_like(pair)
    return jnp.concatenate(
        [jnp.where(at < HEAD_DIM, pair, zero), jnp.where(at < HEAD_DIM, zero, pair)], axis=axis
    )


def own_parts(x):
    queries = x.shape[1] // 2
    return jnp.concatenate([x[:HEAD_DIM, :queries], x[HEAD_DIM:, queries:]], axis=0)


def forward_kernel(
    count_ref, place_ref, query_ref, key_ref, value_ref, left_ref, right_ref, attended_ref, log_ref
):
    queries, model = query_ref.shape
    gaps = distances(place_ref[0], queries + 2 * FRAME, queries)
    for pair in range(model // PAIR):
        lanes = slice(pair * PAIR, (pair + 1) * PAIR)
        keys = window(left_ref, key_ref, right_ref, 0, lanes)
        values = window(left_ref, value_ref, right_ref, 1, lanes)
        scores = dot(keys, spread(query_ref[:, lanes], 0), NT)
        scores = masked(scores, gaps, count_ref, pair, queries)
        top = jnp.max(scores, axis=0, keepdims=True)
        raw = jnp.exp2(scores - top)
        total = jnp.sum(raw, axis=0, keepdims=True)
        rounded = (raw * (1.0 / total)).astype(BF16)
        attended_ref[lanes, :] = own_parts(dot(values.T, rounded, NN)).astype(BF16)
        log_ref[pair] = top + jnp.log2(total)


def backward_kernel(
    count_ref, place_ref, query_ref, key_ref, value_ref, left_ref, right_ref, attended_ref, log_ref,
    mixed_ref, query_grad_ref, key_own_ref, value_own_ref, to_left_ref, to_right_ref,
):
    queries, model = query_ref.shape
    gaps = distances(place_ref[0], queries + 2 * FRAME, queries)
    for pair in range(model // PAIR):
        lanes = slice(pair * PAIR, (pair + 1) * PAIR)
        keys = window(left_ref, key_ref, right_ref, 0, lanes)
        values = window(left_ref, value_ref, right_ref, 1, lanes)
        query = spread(query_ref[:, lanes], 0)
        up_t = up_rows(mixed_ref, pair)
        up = spread(up_t, 1)
        scores = masked(dot(keys, query, NT), gaps, count_ref, pair, queries)
        weights = jnp.exp2(scores - log_ref[pair])
        product = up_t.astype(F32) * attended_ref[lanes, :].astype(F32)
        inner = jnp.concatenate(
            [
                jnp.sum(product[:HEAD_DIM], axis=0, keepdims=True),
                jnp.sum(product[HEAD_DIM:], axis=0, keepdims=True),
            ],
            axis=1,
        )
        prob_grad = dot(values, up, NN)
        score_grad = (weights * (prob_grad - inner)).astype(BF16)
        query_grad = own_parts(dot(keys.T, score_grad, NN)) * SCORE_SCALE
        query_grad_ref[:, lanes] = query_grad.T.astype(BF16)
        key_grad = dot(score_grad, query, NN) * SCORE_SCALE
        value_grad = dot(weights.astype(BF16), up, NT)
        for part, (grad, own_ref) in enumerate(
            ((key_grad, key_own_ref), (value_grad, value_own_ref))
        ):
            to_left_ref[part, :, lanes] = grad[:FRAME].astype(BF16)
            own_ref[:, lanes] = grad[FRAME : FRAME + queries]
            to_right_ref[part, :, lanes] = grad[FRAME + queries :].astype(BF16)


def finish_kernel(key_own_ref, value_own_ref, left_ref, right_ref, key_ref, value_ref):
    for part, (own_ref, out_ref) in enumerate(((key_own_ref, key_ref), (value_own_ref, value_ref))):
        out_ref[:FRAME, :] = (own_ref[:FRAME, :] + left_ref[part].astype(F32)).astype(BF16)
        out_ref[FRAME:, :] = (own_ref[FRAME:, :] + right_ref[part].astype(F32)).astype(BF16)


def up_rows(ref, pair):
    width = ref.shape[1] // 2
    pieces = []
    at = pair * PAIR
    while at < (pair + 1) * PAIR:
        end = min((pair + 1) * PAIR, (at // width + 1) * width)
        first = width + at % width
        pieces.append(ref[at // width, first : first + end - at, :])
        at = end
    return pieces[0] if len(pieces) == 1 else jnp.concatenate(pieces, axis=0)


def weight_kernel(mixed_ref, grad_ref, out_ref, *, column_parts):
    peers, rows, _ = mixed_ref.shape
    attended = jnp.concatenate([mixed_ref[peer, : rows // 2, :] for peer in range(peers)], axis=1)
    term = dot(attended, grad_ref[...], NN).T
    dp_size = out_ref.shape[0]
    wide = term.shape[0] // (dp_size * column_parts)
    high = wide * column_parts
    for peer in range(dp_size):
        block = jnp.concatenate(
            [
                term[(part * dp_size + peer) * wide : (part * dp_size + peer + 1) * wide]
                for part in range(column_parts)
            ],
            axis=0,
        )
        out_ref[peer, :high, :] = block[:, :128].astype(BF16)
        out_ref[peer, high:, :] = jnp.concatenate(
            [block[: high // 2, 128:], block[high // 2 :, 128:]], axis=1
        ).astype(BF16)


def sum_kernel(x_ref, out_ref):
    column_parts = out_ref.shape[0]
    high = x_ref.shape[1] * 2 // 3
    wide = high // column_parts
    total = x_ref[0].astype(F32)
    for peer in range(1, x_ref.shape[0]):
        total = total + x_ref[peer].astype(F32)
    rest = jnp.concatenate([total[high:, :64], total[high:, 64:]], axis=0)
    for part in range(column_parts):
        at = part * wide
        first = jnp.concatenate([rest[at : at + 8], rest[at + 8 : at + 16]], axis=1)
        last = jnp.concatenate([rest[at + 16 : at + 24], jnp.zeros((8, 64), F32)], axis=1)
        out_ref[part] = jnp.concatenate([total[at : at + wide], first, last], axis=0).astype(BF16)


def mean_kernel(x_ref, out_ref, *, clips):
    total = x_ref[0].astype(F32)
    for part in range(1, x_ref.shape[0]):
        total = total + x_ref[part].astype(F32)
    rest = jnp.concatenate([total[24:32, :64], total[24:32, 64:], total[32:, :64]], axis=0)
    total = jnp.concatenate([total[:24], rest], axis=1)
    out_ref[...] = total * (1.0 / clips)


def upstream_kernel(weight_ref, grad_ref, attended_ref, out_ref):
    up = dot(weight_ref[...], grad_ref[...], NT).astype(BF16)
    peers, both, tokens = out_ref.shape
    width = both // 2
    for peer in range(peers):
        out_ref[peer, :width, :] = attended_ref[peer * width : (peer + 1) * width, :]
        out_ref[peer, width:, :] = up[:, peer * tokens : (peer + 1) * tokens]


def layer_kernel(attended_ref, weight_ref, out_ref):
    out_ref[...] = dot(attended_ref[...].T, weight_ref[...], NN).astype(BF16)


def per_device(query_in, key_in, value_in, out_grad, out_weight, key_tiles, key_count):
    seq_size = lax.axis_size("seq")
    fsdp_size = lax.axis_size("fsdp")
    dp_size = lax.axis_size("dp")
    query, key, value, grad = query_in[0], key_in[0], value_in[0], out_grad[0]
    tokens, model = query.shape
    width = model // seq_size
    heads = model // HEAD_DIM
    columns = model // (fsdp_size * dp_size)
    shape = jax.ShapeDtypeStruct
    place = lax.axis_index("seq").astype(jnp.int32).reshape(1)
    upward = [(i, i + 1) for i in range(seq_size - 1)]
    downward = [(i + 1, i) for i in range(seq_size - 1)]

    grad_all = lax.all_gather(grad, "seq", axis=0, tiled=True)
    left = lax.ppermute(jnp.stack([key[FRAME:], value[FRAME:]]), "seq", upward)
    right = lax.ppermute(jnp.stack([key[:FRAME], value[:FRAME]]), "seq", downward)
    weight_copies, own_count = call(
        spread_weight_kernel,
        (
            shape((fsdp_size, width * out_weight.shape[1] // 128, 128), BF16),
            shape(key_count.shape[1:], key_count.dtype),
        ),
        (out_weight, key_count[0]),
    )
    weight_copies = lax.all_to_all(weight_copies, "fsdp", split_axis=0, concat_axis=0, tiled=True)
    counts = lax.all_gather(own_count, "seq", axis=0, tiled=True)
    attended, log_total = call(
        forward_kernel,
        (
            shape((model, tokens), BF16),
            shape((heads // 2, 1, 2 * tokens), F32),
        ),
        (counts, place, query, key, value, left, right),
        scalars=2,
        us=7,
    )
    row_weight = call(
        join_weight_kernel, shape((width, model), BF16), (weight_copies,), after=(log_total,)
    )
    full_weight = lax.all_gather(row_weight, "seq", axis=0, tiled=True)
    mixed = call(
        upstream_kernel,
        shape((seq_size, 2 * width, tokens), BF16),
        (row_weight, grad_all, attended),
        us=4,
    )
    mixed = lax.all_to_all(mixed, "seq", split_axis=0, concat_axis=0, tiled=True)

    term = call(
        functools.partial(weight_kernel, column_parts=fsdp_size),
        shape((dp_size, fsdp_size * columns * width // 128, 128), BF16),
        (mixed, grad_all),
        us=4,
    )
    query_grad, key_own, value_own, to_left, to_right = call(
        backward_kernel,
        (
            shape((tokens, model), BF16),
            shape((tokens, model), F32),
            shape((tokens, model), F32),
            shape((2, FRAME, model), BF16),
            shape((2, FRAME, model), BF16),
        ),
        (counts, place, query, key, value, left, right, attended, log_total, mixed),
        scalars=2,
        us=7,
    )
    term = lax.all_to_all(term, "dp", split_axis=0, concat_axis=0, tiled=True)
    term = call(sum_kernel, shape((fsdp_size, columns + 16, 128), BF16), (term,), after=(to_left,))
    term = lax.all_to_all(term, "fsdp", split_axis=0, concat_axis=0, tiled=True)
    from_left = lax.ppermute(to_right, "seq", upward)
    from_right = lax.ppermute(to_left, "seq", downward)
    key_grad, value_grad = call(
        finish_kernel, (shape((tokens, model), BF16),) * 2, (key_own, value_own, from_left, from_right)
    )
    layer_out = call(layer_kernel, shape((tokens, model), BF16), (attended, full_weight), us=4)
    weight_grad = call(
        functools.partial(mean_kernel, clips=fsdp_size * dp_size),
        shape((columns, width), F32),
        (term,),
        after=(key_grad, layer_out),
    ).T

    return (layer_out[None], query_grad[None], key_grad[None], value_grad[None], weight_grad)


def solution(mesh):
    clips = ("fsdp", "dp")
    tokens = P(clips, "seq", None)
    return jax.shard_map(
        per_device,
        mesh=mesh,
        in_specs=(
            tokens,
            tokens,
            tokens,
            tokens,
            P("seq", "fsdp"),
            P(clips, "seq", None, None),
            P(clips, "seq", None),
        ),
        out_specs=(tokens, tokens, tokens, tokens, P("seq", clips)),
        check_vma=False,
    )
```

time: 191 us -> 147 us (0.77)
  blocking collectives: 86.7 us -> 39.3 us
  starting transfers between devices: 24.3 us -> 42.8 us
  waiting for transfers between devices: 24.4 us -> 7.11 us
    all_gather x2 -> x1, blocking collectives: 47.2 us -> 22.2 us  [per_device(): counts = lax.all_gather(own_count, 'seq', axis=0, tiled=True)]
    all_to_all x2 -> x1, blocking collectives: 39.5 us -> 17.1 us  [per_device(): lax.all_to_all(mixed, 'seq', split_axis=0, concat_axis=0, tiled=True)]
    all_to_all x3, waiting for transfers between devices: 23.7 us -> 6.38 us  [the longest x1 6.38 us: per_device(): term = lax.all_to_all(term, 'fsdp', split_axis=0, concat_axis=0, tiled=True)]
    ppermute x0 -> x4, starting transfers between devices: none -> 11.6 us  [the longest x1 4.05 us: per_device(): left = lax.ppermute(jnp.stack([key[FRAME:], value[FRAME:]]), 'seq', upward)]
    all_to_all x3, starting transfers between devices: 24.2 us -> 31.1 us  [the longest x1 15.7 us: per_device(): lax.all_to_all(weight_copies, 'fsdp', split_axis=0, concat_axis=0, tiled=...]
    unnamed x7 -> x20, local copies, waits for them, and re-layouts: 2.43 us -> 5.95 us
    pallas_call x8 -> x10, Pallas kernels: 35.7 us -> 35.9 us  [call(): pl.pallas_call(body, out_shape=out_shape, in_specs=[pl.BlockSpec(memory_s...]
  transfers between devices with their start and end apart: 5 -> 9, of which waited for: 3 -> 1; matrix products, arithmetic and copies ran while one was open for 2% -> 1% of each run, Pallas kernels for 17% -> 24%
where the time goes in v2:
time: 147 us; the launch traced here: 145 us
  starting transfers between devices  42.8 us (29%)
  blocking collectives  39.3 us (27%)
  Pallas kernels  35.9 us (24%)
  between operations  14.2 us (10%)
  waiting for transfers between devices  7.11 us (5%)
  local copies, waits for them, and re-layouts  6.01 us (4%)
    pallas_call x10, Pallas kernels, call(): pl.pallas_call(body, out_shape=out_shape, in_specs=[pl.BlockSpec(memory_s...  35.9 us
    all_gather x1, blocking collectives, per_device(): counts = lax.all_gather(own_count, 'seq', axis=0, tiled=True)  22.2 us
    all_to_all x1, blocking collectives, per_device(): lax.all_to_all(mixed, 'seq', split_axis=0, concat_axis=0, tiled=True)  17.1 us
    all_to_all x1, starting transfers between devices, per_device(): lax.all_to_all(weight_copies, 'fsdp', split_axis=0, concat_axis=0, tiled=...  15.7 us
    all_to_all x1, starting transfers between devices, per_device(): term = lax.all_to_all(term, 'fsdp', split_axis=0, concat_axis=0, tiled=True)  11.4 us
    all_to_all x1, waiting for transfers between devices, per_device(): term = lax.all_to_all(term, 'fsdp', split_axis=0, concat_axis=0, tiled=True)  6.38 us
    unnamed x20, local copies, waits for them, and re-layouts  5.95 us
    ppermute x1, starting transfers between devices, per_device(): left = lax.ppermute(jnp.stack([key[FRAME:], value[FRAME:]]), 'seq', upward)  4.05 us
  transfers between devices with their start and end apart: 9, of which 1 were waited for; matrix products, arithmetic and copies ran while one was open for 1% of the time, Pallas kernels for 24%

profile of v2, /device:TPU:1, one launch (start us, length us, event | category | flops | bytes accessed | tf_op | source)
XLA Modules:
  0.0 145.4 jit_solution(13891320178681723465)
XLA Ops:
  7.2 0.0 copy-start.2
  7.2 0.0 copy-start.3
  7.2 0.0 all-gather.7.cloned.1.call-start
  7.2 0.7 all-gather.7.cloned.1.call-update
  7.9 1.3 copy.13
  9.2 1.8 %shard_map.101 = (bf16[16,144,128]{2,1,0:T(8,128)(2,1)}, s32[3,32]{1,0:T(4,128)}) custom-call(bf16[192,96]{1,0:T(8,128)(2,1)} %refs_0_.1, s32[3,32]{1,0:T(4,128)} %bitcast.19), custom_call_target="tpu_custom_call" | custom-call | flops 2000000000 | bytes 6000000 | tf_op jit(solution)/shard_map/pallas_call | solution.py:36
  11.0 15.7 %all-to-all-start = ((bf16[16,144,128]{2,1,0:T(8,128)(2,1)}), bf16[16,144,128]{2,1,0:T(8,128)(2,1)S(1)}, u32[]{:S(2)}, u32[]{:S(2)}) async-start(bf16[16,144,128]{2,1,0:T(8,128)(2,1)} %get-tuple-element.19), calls=%async_computation | async-start | bytes 1179648 | tf_op jit(solution)/shard_map/all_to_all | solution.py:273
  26.8 0.0 all-gather.5.cloned.1.call-start
  26.8 0.0 copy-done.2
  26.8 0.0 copy-done.3
  26.8 0.1 fusion
  26.9 4.0 %collective-permute-start = (bf16[2,64,1536]{2,1,0:T(8,128)(2,1)S(1)}, bf16[2,64,1536]{2,1,0:T(8,128)(2,1)S(1)}, u32[]{:S(2)}, u32[]{:S(2)}) collective-permute-start(bf16[2,64,1536]{2,1,0:T(8,128)(2,1)S(1)} %pad_maximum_fusion), channel_id=1, source_target_pairs={{0,64},{64,128},{128,192},{192,256},{256,320},{320,384},{384,448},... | collective-permute-start | bytes 1179656 | tf_op jit(solution)/shard_map/ppermute | solution.py:263
  31.0 1.9 %collective-permute-start.1 = (bf16[2,64,1536]{2,1,0:T(8,128)(2,1)S(1)}, bf16[2,64,1536]{2,1,0:T(8,128)(2,1)S(1)}, u32[]{:S(2)}, u32[]{:S(2)}) collective-permute-start(bf16[2,64,1536]{2,1,0:T(8,128)(2,1)S(1)} %pad_maximum_fusion.1), channel_id=1, source_target_pairs={{64,0},{128,64},{192,128},{256,192},{320,256},{384,320},{448,384},... | collective-permute-start | bytes 1179656 | tf_op jit(solution)/shard_map/ppermute | solution.py:264
  33.0 22.2 %all-gather.1 = s32[8,3,32]{2,1,0:T(4,128)S(1)} all-gather(s32[1,3,32]{2,1,0:T(4,128)} %bitcast.18), channel_id=1, replica_groups=mesh['seq'=8,'fsdp'=16,'dp'=4] {'seq'}, dimensions={0}, use_global_device_ids=true | all-gather | bytes 3456 | tf_op jit(solution)/shard_map/all_gather | solution.py:274
  55.1 0.6 reshape.24.refs_0_
  55.7 0.0 collective-permute-done.refs_5_
  55.7 0.0 copy-start.5
  55.7 0.0 collective-permute-done.1.refs_6_
  55.8 0.0 copy-start.6
  55.8 0.7 copy-done.5
  56.5 0.1 copy-done.6
  56.6 6.4 %shard_map.102 = (bf16[1536,128]{1,0:T(8,128)(2,1)}, f32[12,1,256]{2,1,0:T(1,128)}) custom-call(s32[24,32]{1,0:T(8,128)} %reshape.24.refs_0_, s32[1]{0:T(128)} %bitcast.1.refs_1_, bf16[128,1536]{1,0:T(8,128)(2,1)} %bitcast.22, bf16[128,1536]{1,0:T(8,128)(2,1)} %bitcast.14, bf16[128,1536]{1,0:T(8,128)(2,1)} %bitcast.16, bf16[2,64,1536]{2,1,0:T(8,128)(2,1)} %copy-done.5, ...), custom_call_target="tpu_custom_call" | custom-call | flops 7000000000 | bytes 21000000 | tf_op jit(solution)/shard_map/pallas_call | solution.py:36
  63.0 0.0 all-to-all-done.refs_1_
  63.0 0.0 copy-start
  63.0 0.9 copy-done
  63.9 2.4 %shard_map.103.refs_0_ = bf16[192,1536]{1,0:T(8,128)(2,1)} custom-call(f32[12,1,256]{2,1,0:T(1,128)} %get-tuple-element.18.refs_0_.refs_8_, bf16[16,144,128]{2,1,0:T(8,128)(2,1)} %copy-done), custom_call_target="tpu_custom_call" | custom-call | flops 2000000000 | bytes 6000000 | tf_op jit(solution)/shard_map/pallas_call | solution.py:36
  66.3 0.0 all-gather.5.cloned.1.call-update
  66.3 0.0 all-gather.7.cloned.1.call-done
  66.3 4.2 %shard_map.105 = bf16[8,384,128]{2,1,0:T(8,128)(2,1)} custom-call(bf16[192,1536]{1,0:T(8,128)(2,1)} %shard_map.103.refs_0_, bf16[1024,1536]{1,0:T(8,128)(2,1)} %bitcast.20, bf16[1536,128]{1,0:T(8,128)(2,1)} %get-tuple-element.17.refs_0_.refs_2_.refs_7_), custom_call_target="tpu_custom_call" | custom-call | flops 4000000000 | bytes 12000000 | tf_op jit(solution)/shard_map/pallas_call | solution.py:36
  70.5 17.1 %all_to_all.20.refs_9_.refs_0_ = bf16[8,384,128]{2,1,0:T(8,128)(2,1)} all-to-all(bf16[8,384,128]{2,1,0:T(8,128)(2,1)} %shard_map.105), channel_id=1, replica_groups=mesh['seq'=8,'fsdp'=16,'dp'=4] {'seq'}, dimensions={0} | all-to-all | bytes 1572864 | tf_op jit(solution)/shard_map/all_to_all | solution.py:295
  87.6 3.9 %shard_map.108 = bf16[4,576,128]{2,1,0:T(8,128)(2,1)} custom-call(bf16[8,384,128]{2,1,0:T(8,128)(2,1)} %all_to_all.20.refs_9_.refs_0_, bf16[1024,1536]{1,0:T(8,128)(2,1)} %bitcast.21), custom_call_target="tpu_custom_call" | custom-call | flops 4000000000 | bytes 12000000 | tf_op jit(solution)/shard_map/pallas_call | solution.py:36
  91.6 4.0 %all-to-all-start.2 = ((bf16[4,576,128]{2,1,0:T(8,128)(2,1)}), bf16[4,576,128]{2,1,0:T(8,128)(2,1)S(1)}, u32[]{:S(2)}, u32[]{:S(2)}) async-start(bf16[4,576,128]{2,1,0:T(8,128)(2,1)} %shard_map.108), calls=%async_computation.2 | async-start | bytes 1179648 | tf_op jit(solution)/shard_map/all_to_all | solution.py:316
  95.5 7.1 %shard_map.106 = (bf16[128,1536]{1,0:T(8,128)(2,1)}, f32[128,1536]{1,0:T(8,128)}, f32[128,1536]{1,0:T(8,128)}, bf16[2,64,1536]{2,1,0:T(8,128)(2,1)}, bf16[2,64,1536]{2,1,0:T(8,128)(2,1)}) custom-call(s32[24,32]{1,0:T(8,128)} %reshape.24.refs_0_, s32[1]{0:T(128)} %bitcast.1.refs_1_, bf16[128,1536]{1,0:T(8,128)(2,1)} %bitcast.23, bf16[128,1536]{1,0:T(8,128)(2,1)} %bitcast.15, ...), custom_call_target="tpu_custom_call" | custom-call | flops 7000000000 | bytes 21000000 | tf_op jit(solution)/shard_map/pallas_call | solution.py:36
  102.7 3.8 %collective-permute-start.2 = (bf16[2,64,1536]{2,1,0:T(8,128)(2,1)}, bf16[2,64,1536]{2,1,0:T(8,128)(2,1)S(1)}, u32[]{:S(2)}, u32[]{:S(2)}) collective-permute-start(bf16[2,64,1536]{2,1,0:T(8,128)(2,1)} %get-tuple-element.23), channel_id=1, source_target_pairs={{0,64},{64,128},{128,192},{192,256},{256,320},{320,384},{384,448},... | collective-permute-start | bytes 1179656 | tf_op jit(solution)/shard_map/ppermute | solution.py:319
  106.4 1.9 %collective-permute-start.3 = (bf16[2,64,1536]{2,1,0:T(8,128)(2,1)}, bf16[2,64,1536]{2,1,0:T(8,128)(2,1)S(1)}, u32[]{:S(2)}, u32[]{:S(2)}) collective-permute-start(bf16[2,64,1536]{2,1,0:T(8,128)(2,1)} %get-tuple-element.24.refs_0_), channel_id=1, source_target_pairs={{64,0},{128,64},{192,128},{256,192},{320,256},{384,320},{448,384},... | collective-permute-start | bytes 1179656 | tf_op jit(solution)/shard_map/ppermute | solution.py:320
  108.3 0.0 all-to-all-done.2.refs_1_
  108.4 0.0 copy-start.1
  108.4 0.8 copy-done.1
  109.2 1.9 %shard_map.109 = bf16[16,40,128]{2,1,0:T(8,128)(2,1)} custom-call(bf16[2,64,1536]{2,1,0:T(8,128)(2,1)} %get-tuple-element.24.refs_0_, bf16[4,576,128]{2,1,0:T(8,128)(2,1)} %copy-done.1), custom_call_target="tpu_custom_call" | custom-call | flops 2000000000 | bytes 6000000 | tf_op jit(solution)/shard_map/pallas_call | solution.py:36
  111.1 11.4 %all-to-all-start.3 = ((bf16[16,40,128]{2,1,0:T(8,128)(2,1)}), bf16[16,40,128]{2,1,0:T(8,128)(2,1)S(1)}, u32[]{:S(2)}, u32[]{:S(2)}) async-start(bf16[16,40,128]{2,1,0:T(8,128)(2,1)} %shard_map.109), calls=%async_computation.3 | async-start | bytes 327680 | tf_op jit(solution)/shard_map/all_to_all | solution.py:318
  122.4 0.0 collective-permute-done.2.refs_2_
  122.5 0.0 copy-start.7
  122.5 0.0 collective-permute-done.3.refs_3_
  122.5 0.0 copy-start.8
  122.5 0.7 copy-done.7
  123.2 0.1 copy-done.8
  123.3 2.5 %shard_map.107 = (bf16[128,1536]{1,0:T(8,128)(2,1)}, bf16[128,1536]{1,0:T(8,128)(2,1)}) custom-call(f32[128,1536]{1,0:T(8,128)} %get-tuple-element.21.refs_0_, f32[128,1536]{1,0:T(8,128)} %get-tuple-element.22.refs_1_, bf16[2,64,1536]{2,1,0:T(8,128)(2,1)} %copy-done.7, bf16[2,64,1536]{2,1,0:T(8,128)(2,1)} %copy-done.8), custom_call_target="tpu_custom_call" | custom-call | flops 2000000000 | bytes 6000000 | tf_op jit(solution)/shard_map/pallas_call | solution.py:36
  125.9 0.0 all-gather.5.cloned.1.call-done.refs_1_
  125.9 4.0 %shard_map.104.refs_1_ = bf16[128,1536]{1,0:T(8,128)(2,1)} custom-call(bf16[1536,128]{1,0:T(8,128)(2,1)} %get-tuple-element.17.refs_0_.refs_2_.refs_7_, bf16[1536,1536]{1,0:T(8,128)(2,1)} %all-gather.5.cloned.1.call-done.refs_1_), custom_call_target="tpu_custom_call" | custom-call | flops 4000000000 | bytes 12000000 | tf_op jit(solution)/shard_map/pallas_call | solution.py:36
  129.9 6.4 %all-to-all-done.3.refs_2_ = bf16[16,40,128]{2,1,0:T(8,128)(2,1)S(1)} async-done(((bf16[16,40,128]{2,1,0:T(8,128)(2,1)}), bf16[16,40,128]{2,1,0:T(8,128)(2,1)S(1)}, u32[]{:S(2)}, u32[]{:S(2)}) %all-to-all-start.3) | async-done | bytes 163872 | tf_op jit(solution)/shard_map/all_to_all | solution.py:318
  136.3 0.0 copy-start.4
  136.3 0.7 copy-done.4
  136.9 1.6 %shard_map.110 = f32[24,192]{1,0:T(8,128)} custom-call(bf16[128,1536]{1,0:T(8,128)(2,1)} %get-tuple-element.25.refs_0_, bf16[128,1536]{1,0:T(8,128)(2,1)} %shard_map.104.refs_1_, bf16[16,40,128]{2,1,0:T(8,128)(2,1)} %copy-done.4), custom_call_target="tpu_custom_call" | custom-call | flops 2000000000 | bytes 6000000 | tf_op jit(solution)/shard_map/pallas_call | solution.py:36
  (2 shorter events, 0.1 us)
Async XLA Ops:
  7.2 19.6 %copy-start.2 = (bf16[1,128,1536]{2,1,0:T(8,128)(2,1)S(1)}, bf16[1,128,1536]{2,1,0:T(8,128)(2,1)}, u32[]{:S(2)}) copy-start(bf16[1,128,1536]{2,1,0:T(8,128)(2,1)} %param.8) | copy-start | bytes 1179652
  7.2 19.6 %copy-start.3 = (bf16[1,128,1536]{2,1,0:T(8,128)(2,1)S(1)}, bf16[1,128,1536]{2,1,0:T(8,128)(2,1)}, u32[]{:S(2)}) copy-start(bf16[1,128,1536]{2,1,0:T(8,128)(2,1)} %param.9) | copy-start | bytes 1179652
  7.2 59.1 %all-gather.7.cloned.1.call-start = ((), (), s32[]{:S(2)}) async-start(), calls=%async_computation.5 | async-start | bytes 3538944 | tf_op jit(solution)/shard_map/all_gather | solution.py:262
  11.0 52.0 %all-to-all-start = ((bf16[16,144,128]{2,1,0:T(8,128)(2,1)}), bf16[16,144,128]{2,1,0:T(8,128)(2,1)S(1)}, u32[]{:S(2)}, u32[]{:S(2)}) async-start(bf16[16,144,128]{2,1,0:T(8,128)(2,1)} %get-tuple-element.19), calls=%async_computation | async-start | bytes 1179648 | tf_op jit(solution)/shard_map/all_to_all | solution.py:273
  26.8 99.1 %all-gather.5.cloned.1.call-start = ((), (), s32[]{:S(2)}) async-start(), calls=%async_computation.4 | async-start | bytes 5308416 | tf_op jit(solution)/shard_map/all_gather | solution.py:288
  26.9 28.8 %collective-permute-start = (bf16[2,64,1536]{2,1,0:T(8,128)(2,1)S(1)}, bf16[2,64,1536]{2,1,0:T(8,128)(2,1)S(1)}, u32[]{:S(2)}, u32[]{:S(2)}) collective-permute-start(bf16[2,64,1536]{2,1,0:T(8,128)(2,1)S(1)} %pad_maximum_fusion), channel_id=1, source_target_pairs={{0,64},{64,128},{128,192},{192,256},{256,320},{320,384},{384,448},... | collective-permute-start | bytes 1179656 | tf_op jit(solution)/shard_map/ppermute | solution.py:263
  31.0 24.7 %collective-permute-start.1 = (bf16[2,64,1536]{2,1,0:T(8,128)(2,1)S(1)}, bf16[2,64,1536]{2,1,0:T(8,128)(2,1)S(1)}, u32[]{:S(2)}, u32[]{:S(2)}) collective-permute-start(bf16[2,64,1536]{2,1,0:T(8,128)(2,1)S(1)} %pad_maximum_fusion.1), channel_id=1, source_target_pairs={{64,0},{128,64},{192,128},{256,192},{320,256},{384,320},{448,384},... | collective-permute-start | bytes 1179656 | tf_op jit(solution)/shard_map/ppermute | solution.py:264
  55.7 0.7 copy-start.5
  55.8 0.9 copy-start.6
  63.0 0.9 copy-start
  91.6 16.8 %all-to-all-start.2 = ((bf16[4,576,128]{2,1,0:T(8,128)(2,1)}), bf16[4,576,128]{2,1,0:T(8,128)(2,1)S(1)}, u32[]{:S(2)}, u32[]{:S(2)}) async-start(bf16[4,576,128]{2,1,0:T(8,128)(2,1)} %shard_map.108), calls=%async_computation.2 | async-start | bytes 1179648 | tf_op jit(solution)/shard_map/all_to_all | solution.py:316
  102.7 19.8 %collective-permute-start.2 = (bf16[2,64,1536]{2,1,0:T(8,128)(2,1)}, bf16[2,64,1536]{2,1,0:T(8,128)(2,1)S(1)}, u32[]{:S(2)}, u32[]{:S(2)}) collective-permute-start(bf16[2,64,1536]{2,1,0:T(8,128)(2,1)} %get-tuple-element.23), channel_id=1, source_target_pairs={{0,64},{64,128},{128,192},{192,256},{256,320},{320,384},{384,448},... | collective-permute-start | bytes 1179656 | tf_op jit(solution)/shard_map/ppermute | solution.py:319
  106.4 16.1 %collective-permute-start.3 = (bf16[2,64,1536]{2,1,0:T(8,128)(2,1)}, bf16[2,64,1536]{2,1,0:T(8,128)(2,1)S(1)}, u32[]{:S(2)}, u32[]{:S(2)}) collective-permute-start(bf16[2,64,1536]{2,1,0:T(8,128)(2,1)} %get-tuple-element.24.refs_0_), channel_id=1, source_target_pairs={{64,0},{128,64},{192,128},{256,192},{320,256},{384,320},{448,384},... | collective-permute-start | bytes 1179656 | tf_op jit(solution)/shard_map/ppermute | solution.py:320
  108.4 0.8 copy-start.1
  111.1 25.2 %all-to-all-start.3 = ((bf16[16,40,128]{2,1,0:T(8,128)(2,1)}), bf16[16,40,128]{2,1,0:T(8,128)(2,1)S(1)}, u32[]{:S(2)}, u32[]{:S(2)}) async-start(bf16[16,40,128]{2,1,0:T(8,128)(2,1)} %shard_map.109), calls=%async_computation.3 | async-start | bytes 327680 | tf_op jit(solution)/shard_map/all_to_all | solution.py:318
  122.5 0.7 copy-start.7
  122.5 0.9 copy-start.8
  136.3 0.7 copy-start.4
Sparse Core Ops, SparseCore 0:
  10.1 44.2 all-gather.6
  66.4 41.9 all-gather.4

commit v3 on v2

--- a/solution.py
+++ b/solution.py
@@ -47,7 +47,22 @@
     )(*after, *operands)
 
 
-def spread_weight_kernel(weight_ref, count_ref, out_ref, count_out_ref):
+def held_until(x, after):
+    anywhere = pl.BlockSpec(memory_space=pl.ANY)
+
+    def body(*refs):
+        pass
+
+    return pl.pallas_call(
+        body,
+        out_shape=jax.ShapeDtypeStruct(x.shape, x.dtype),
+        in_specs=[anywhere] * (1 + len(after)),
+        out_specs=anywhere,
+        input_output_aliases={0: 0},
+    )(x, *after)
+
+
+def spread_weight_kernel(weight_ref, out_ref):
     rows, width = weight_ref.shape
     high = rows * width // 128
     piece = 128 - width
@@ -55,7 +70,6 @@
     dense = jnp.concatenate([weight_ref[:high, :], jnp.concatenate(pieces, axis=0)], axis=1)
     for peer in range(out_ref.shape[0]):
         out_ref[peer] = dense
-    count_out_ref[...] = count_ref[...]
 
 
 def join_weight_kernel(x_ref, out_ref):
@@ -233,7 +247,7 @@
 
 
 def upstream_kernel(weight_ref, grad_ref, attended_ref, out_ref):
-    up = dot(weight_ref[...], grad_ref[...], NT).astype(BF16)
+    up = dot(grad_ref[...], weight_ref[...], NT).T.astype(BF16)
     peers, both, tokens = out_ref.shape
     width = both // 2
     for peer in range(peers):
@@ -262,16 +276,15 @@
     grad_all = lax.all_gather(grad, "seq", axis=0, tiled=True)
     left = lax.ppermute(jnp.stack([key[FRAME:], value[FRAME:]]), "seq", upward)
     right = lax.ppermute(jnp.stack([key[:FRAME], value[:FRAME]]), "seq", downward)
-    weight_copies, own_count = call(
+    weight_copies = call(
         spread_weight_kernel,
-        (
-            shape((fsdp_size, width * out_weight.shape[1] // 128, 128), BF16),
-            shape(key_count.shape[1:], key_count.dtype),
-        ),
-        (out_weight, key_count[0]),
-    )
+        shape((fsdp_size, width * out_weight.shape[1] // 128, 128), BF16),
+        (out_weight,),
+    )
+    own_count = held_until(key_count[0], (weight_copies,))
     weight_copies = lax.all_to_all(weight_copies, "fsdp", split_axis=0, concat_axis=0, tiled=True)
     counts = lax.all_gather(own_count, "seq", axis=0, tiled=True)
+
     attended, log_total = call(
         forward_kernel,
         (
@@ -314,10 +327,10 @@
         us=7,
     )
     term = lax.all_to_all(term, "dp", split_axis=0, concat_axis=0, tiled=True)
-    term = call(sum_kernel, shape((fsdp_size, columns + 16, 128), BF16), (term,), after=(to_left,))
-    term = lax.all_to_all(term, "fsdp", split_axis=0, concat_axis=0, tiled=True)
-    from_left = lax.ppermute(to_right, "seq", upward)
-    from_right = lax.ppermute(to_left, "seq", downward)
+    summed = call(sum_kernel, shape((fsdp_size, columns + 16, 128), BF16), (term,), after=(to_left,))
+    term = lax.all_to_all(summed, "fsdp", split_axis=0, concat_axis=0, tiled=True)
+    from_left = lax.ppermute(held_until(to_right, (summed,)), "seq", upward)
+    from_right = lax.ppermute(held_until(to_left, (summed,)), "seq", downward)
     key_grad, value_grad = call(
         finish_kernel, (shape((tokens, model), BF16),) * 2, (key_own, value_own, from_left, from_right)
     )

time: 147 us -> 146 us (level)
    all_gather x1, blocking collectives: 22.2 us -> 20.3 us  [per_device(): counts = lax.all_gather(own_count, 'seq', axis=0, tiled=True)]
    unnamed x20 -> x22, local copies, waits for them, and re-layouts: 5.95 us -> 5.28 us
  transfers between devices with their start and end apart: 9 -> 9, of which waited for: 1 -> 2; matrix products, arithmetic and copies ran while one was open for 1% -> 1% of each run, Pallas kernels for 24% -> 24%
where the time goes in v3:
time: 146 us; the launch traced here: 145 us
  starting transfers between devices  43.1 us (30%)
  blocking collectives  38.1 us (26%)
  Pallas kernels  35.8 us (25%)
  between operations  14.2 us (10%)
  waiting for transfers between devices  8.01 us (5%)
  local copies, waits for them, and re-layouts  5.34 us (4%)
    pallas_call x10, Pallas kernels, call(): pl.pallas_call(body, out_shape=out_shape, in_specs=[pl.BlockSpec(memory_s...  35.8 us
    all_gather x1, blocking collectives, per_device(): counts = lax.all_gather(own_count, 'seq', axis=0, tiled=True)  20.3 us
    all_to_all x1, blocking collectives, per_device(): lax.all_to_all(mixed, 'seq', split_axis=0, concat_axis=0, tiled=True)  17.8 us
    all_to_all x1, starting transfers between devices, per_device(): lax.all_to_all(weight_copies, 'fsdp', split_axis=0, concat_axis=0, tiled=...  15.7 us
    all_to_all x1, starting transfers between devices, per_device(): lax.all_to_all(summed, 'fsdp', split_axis=0, concat_axis=0, tiled=True)  10.3 us
    all_to_all x1, waiting for transfers between devices, per_device(): lax.all_to_all(summed, 'fsdp', split_axis=0, concat_axis=0, tiled=True)  6.38 us
    unnamed x22, local copies, waits for them, and re-layouts  5.28 us
    ppermute x1, starting transfers between devices, per_device(): from_left = lax.ppermute(held_until(to_right, (summed,)), 'seq', upward)  4.82 us
  transfers between devices with their start and end apart: 9, of which 2 were waited for; matrix products, arithmetic and copies ran while one was open for 1% of the time, Pallas kernels for 24%

profile of v3, /device:TPU:1, one launch (start us, length us, event | category | flops | bytes accessed | tf_op | source)
XLA Modules:
  0.0 144.7 jit_solution(1381431122994507951)
XLA Ops:
  7.2 0.0 copy-start.2
  7.2 0.0 copy-start.3
  7.2 0.0 all-gather.7.cloned.1.call-start
  7.2 0.7 all-gather.7.cloned.1.call-update
  7.9 0.0 copy-start.5
  7.9 1.8 %shard_map.101.refs_1_ = bf16[16,144,128]{2,1,0:T(8,128)(2,1)} custom-call(bf16[192,96]{1,0:T(8,128)(2,1)} %refs_0_.1), custom_call_target="tpu_custom_call" | custom-call | flops 2000000000 | bytes 6000000 | tf_op jit(solution)/shard_map/pallas_call | solution.py:36
  9.8 15.7 %all-to-all-start = ((bf16[16,144,128]{2,1,0:T(8,128)(2,1)}), bf16[16,144,128]{2,1,0:T(8,128)(2,1)S(1)}, u32[]{:S(2)}, u32[]{:S(2)}) async-start(bf16[16,144,128]{2,1,0:T(8,128)(2,1)} %shard_map.101.refs_1_), calls=%async_computation | async-start | bytes 1179648 | tf_op jit(solution)/shard_map/all_to_all | solution.py:285
  25.5 0.0 all-gather.5.cloned.1.call-start
  25.6 0.0 copy-done.2
  25.6 0.0 copy-done.3
  25.6 0.1 fusion
  25.7 4.0 %collective-permute-start = (bf16[2,64,1536]{2,1,0:T(8,128)(2,1)S(1)}, bf16[2,64,1536]{2,1,0:T(8,128)(2,1)S(1)}, u32[]{:S(2)}, u32[]{:S(2)}) collective-permute-start(bf16[2,64,1536]{2,1,0:T(8,128)(2,1)S(1)} %pad_maximum_fusion), channel_id=1, source_target_pairs={{0,64},{64,128},{128,192},{192,256},{256,320},{320,384},{384,448},... | collective-permute-start | bytes 1179656 | tf_op jit(solution)/shard_map/ppermute | solution.py:277
  29.8 1.9 %collective-permute-start.1 = (bf16[2,64,1536]{2,1,0:T(8,128)(2,1)S(1)}, bf16[2,64,1536]{2,1,0:T(8,128)(2,1)S(1)}, u32[]{:S(2)}, u32[]{:S(2)}) collective-permute-start(bf16[2,64,1536]{2,1,0:T(8,128)(2,1)S(1)} %pad_maximum_fusion.1), channel_id=1, source_target_pairs={{64,0},{128,64},{192,128},{256,192},{320,256},{384,320},{448,384},... | collective-permute-start | bytes 1179656 | tf_op jit(solution)/shard_map/ppermute | solution.py:278
  31.7 0.0 copy-done.5
  31.7 0.6 copy.16
  32.3 20.3 %all-gather.1 = s32[8,3,32]{2,1,0:T(4,128)S(1)} all-gather(s32[1,3,32]{2,1,0:T(4,128)} %bitcast.19), channel_id=1, replica_groups=mesh['seq'=8,'fsdp'=16,'dp'=4] {'seq'}, dimensions={0}, use_global_device_ids=true | all-gather | bytes 3456 | tf_op jit(solution)/shard_map/all_gather | solution.py:286
  52.6 0.6 reshape.24.refs_0_
  53.3 0.0 collective-permute-done.refs_5_
  53.3 0.0 copy-start.6
  53.3 0.0 collective-permute-done.1.refs_6_
  53.3 0.0 copy-start.7
  53.3 0.7 copy-done.6
  54.0 0.1 copy-done.7
  54.1 6.4 %shard_map.103 = (bf16[1536,128]{1,0:T(8,128)(2,1)}, f32[12,1,256]{2,1,0:T(1,128)}) custom-call(s32[24,32]{1,0:T(8,128)} %reshape.24.refs_0_, s32[1]{0:T(128)} %bitcast.1.refs_1_, bf16[128,1536]{1,0:T(8,128)(2,1)} %bitcast.22, bf16[128,1536]{1,0:T(8,128)(2,1)} %bitcast.14, bf16[128,1536]{1,0:T(8,128)(2,1)} %bitcast.16, bf16[2,64,1536]{2,1,0:T(8,128)(2,1)} %copy-done.6, ...), custom_call_target="tpu_custom_call" | custom-call | flops 7000000000 | bytes 21000000 | tf_op jit(solution)/shard_map/pallas_call | solution.py:36
  60.5 0.0 all-to-all-done.refs_1_
  60.5 0.0 copy-start
  60.5 0.9 copy-done
  61.4 2.4 %shard_map.104.refs_0_ = bf16[192,1536]{1,0:T(8,128)(2,1)} custom-call(f32[12,1,256]{2,1,0:T(1,128)} %get-tuple-element.15.refs_0_.refs_8_, bf16[16,144,128]{2,1,0:T(8,128)(2,1)} %copy-done), custom_call_target="tpu_custom_call" | custom-call | flops 2000000000 | bytes 6000000 | tf_op jit(solution)/shard_map/pallas_call | solution.py:36
  63.8 0.0 all-gather.5.cloned.1.call-update
  63.8 0.0 all-gather.7.cloned.1.call-done
  63.8 4.1 %shard_map.106 = bf16[8,384,128]{2,1,0:T(8,128)(2,1)} custom-call(bf16[192,1536]{1,0:T(8,128)(2,1)} %shard_map.104.refs_0_, bf16[1024,1536]{1,0:T(8,128)(2,1)} %bitcast.20, bf16[1536,128]{1,0:T(8,128)(2,1)} %get-tuple-element.14.refs_0_.refs_2_.refs_7_), custom_call_target="tpu_custom_call" | custom-call | flops 4000000000 | bytes 12000000 | tf_op jit(solution)/shard_map/pallas_call | solution.py:36
  67.9 17.8 %all_to_all.20.refs_9_.refs_0_ = bf16[8,384,128]{2,1,0:T(8,128)(2,1)} all-to-all(bf16[8,384,128]{2,1,0:T(8,128)(2,1)} %shard_map.106), channel_id=1, replica_groups=mesh['seq'=8,'fsdp'=16,'dp'=4] {'seq'}, dimensions={0} | all-to-all | bytes 1572864 | tf_op jit(solution)/shard_map/all_to_all | solution.py:308
  85.7 4.0 %shard_map.108 = bf16[4,576,128]{2,1,0:T(8,128)(2,1)} custom-call(bf16[8,384,128]{2,1,0:T(8,128)(2,1)} %all_to_all.20.refs_9_.refs_0_, bf16[1024,1536]{1,0:T(8,128)(2,1)} %bitcast.21), custom_call_target="tpu_custom_call" | custom-call | flops 4000000000 | bytes 12000000 | tf_op jit(solution)/shard_map/pallas_call | solution.py:36
  89.7 4.3 %all-to-all-start.2 = ((bf16[4,576,128]{2,1,0:T(8,128)(2,1)}), bf16[4,576,128]{2,1,0:T(8,128)(2,1)S(1)}, u32[]{:S(2)}, u32[]{:S(2)}) async-start(bf16[4,576,128]{2,1,0:T(8,128)(2,1)} %shard_map.108), calls=%async_computation.2 | async-start | bytes 1179648 | tf_op jit(solution)/shard_map/all_to_all | solution.py:329
  94.0 7.1 %shard_map.107 = (bf16[128,1536]{1,0:T(8,128)(2,1)}, f32[128,1536]{1,0:T(8,128)}, f32[128,1536]{1,0:T(8,128)}, bf16[2,64,1536]{2,1,0:T(8,128)(2,1)}, bf16[2,64,1536]{2,1,0:T(8,128)(2,1)}) custom-call(s32[24,32]{1,0:T(8,128)} %reshape.24.refs_0_, s32[1]{0:T(128)} %bitcast.1.refs_1_, bf16[128,1536]{1,0:T(8,128)(2,1)} %bitcast.23, bf16[128,1536]{1,0:T(8,128)(2,1)} %bitcast.15, ...), custom_call_target="tpu_custom_call" | custom-call | flops 7000000000 | bytes 21000000 | tf_op jit(solution)/shard_map/pallas_call | solution.py:36
  101.1 0.9 all-to-all-done.2.refs_1_
  102.0 0.0 copy-start.1
  102.0 0.8 copy-done.1
  102.8 1.9 %shard_map.109.refs_1_ = bf16[16,40,128]{2,1,0:T(8,128)(2,1)} custom-call(bf16[2,64,1536]{2,1,0:T(8,128)(2,1)} %get-tuple-element.20.refs_0_, bf16[4,576,128]{2,1,0:T(8,128)(2,1)} %copy-done.1), custom_call_target="tpu_custom_call" | custom-call | flops 2000000000 | bytes 6000000 | tf_op jit(solution)/shard_map/pallas_call | solution.py:36
  104.7 4.8 %collective-permute-start.2 = (bf16[2,64,1536]{2,1,0:T(8,128)(2,1)}, bf16[2,64,1536]{2,1,0:T(8,128)(2,1)S(1)}, u32[]{:S(2)}, u32[]{:S(2)}) collective-permute-start(bf16[2,64,1536]{2,1,0:T(8,128)(2,1)} %shard_map.110), channel_id=1, source_target_pairs={{0,64},{64,128},{128,192},{192,256},{256,320},{320,384},{384,448},... | collective-permute-start | bytes 1179656 | tf_op jit(solution)/shard_map/ppermute | solution.py:332
  109.5 1.9 %collective-permute-start.3 = (bf16[2,64,1536]{2,1,0:T(8,128)(2,1)}, bf16[2,64,1536]{2,1,0:T(8,128)(2,1)S(1)}, u32[]{:S(2)}, u32[]{:S(2)}) collective-permute-start(bf16[2,64,1536]{2,1,0:T(8,128)(2,1)} %shard_map.111), channel_id=1, source_target_pairs={{64,0},{128,64},{192,128},{256,192},{320,256},{384,320},{448,384},... | collective-permute-start | bytes 1179656 | tf_op jit(solution)/shard_map/ppermute | solution.py:333
  111.4 10.3 %all-to-all-start.3 = ((bf16[16,40,128]{2,1,0:T(8,128)(2,1)}), bf16[16,40,128]{2,1,0:T(8,128)(2,1)S(1)}, u32[]{:S(2)}, u32[]{:S(2)}) async-start(bf16[16,40,128]{2,1,0:T(8,128)(2,1)} %shard_map.109.refs_1_), calls=%async_computation.3 | async-start | bytes 327680 | tf_op jit(solution)/shard_map/all_to_all | solution.py:331
  121.7 0.0 collective-permute-done.2.refs_2_
  121.8 0.0 copy-start.8
  121.8 0.0 collective-permute-done.3.refs_3_
  121.8 0.0 copy-start.9
  121.8 0.7 copy-done.8
  122.5 0.1 copy-done.9
  122.6 2.5 %shard_map.112 = (bf16[128,1536]{1,0:T(8,128)(2,1)}, bf16[128,1536]{1,0:T(8,128)(2,1)}) custom-call(f32[128,1536]{1,0:T(8,128)} %get-tuple-element.17.refs_0_, f32[128,1536]{1,0:T(8,128)} %get-tuple-element.18.refs_1_, bf16[2,64,1536]{2,1,0:T(8,128)(2,1)} %copy-done.8, bf16[2,64,1536]{2,1,0:T(8,128)(2,1)} %copy-done.9), custom_call_target="tpu_custom_call" | custom-call | flops 2000000000 | bytes 6000000 | tf_op jit(solution)/shard_map/pallas_call | solution.py:36
  125.2 0.0 all-gather.5.cloned.1.call-done.refs_1_
  125.2 4.0 %shard_map.105.refs_1_ = bf16[128,1536]{1,0:T(8,128)(2,1)} custom-call(bf16[1536,128]{1,0:T(8,128)(2,1)} %get-tuple-element.14.refs_0_.refs_2_.refs_7_, bf16[1536,1536]{1,0:T(8,128)(2,1)} %all-gather.5.cloned.1.call-done.refs_1_), custom_call_target="tpu_custom_call" | custom-call | flops 4000000000 | bytes 12000000 | tf_op jit(solution)/shard_map/pallas_call | solution.py:36
  129.2 6.4 %all-to-all-done.3.refs_2_ = bf16[16,40,128]{2,1,0:T(8,128)(2,1)S(1)} async-done(((bf16[16,40,128]{2,1,0:T(8,128)(2,1)}), bf16[16,40,128]{2,1,0:T(8,128)(2,1)S(1)}, u32[]{:S(2)}, u32[]{:S(2)}) %all-to-all-start.3) | async-done | bytes 163872 | tf_op jit(solution)/shard_map/all_to_all | solution.py:331
  135.6 0.0 copy-start.4
  135.6 0.7 copy-done.4
  136.2 1.6 %shard_map.113 = f32[24,192]{1,0:T(8,128)} custom-call(bf16[128,1536]{1,0:T(8,128)(2,1)} %get-tuple-element.21.refs_0_, bf16[128,1536]{1,0:T(8,128)(2,1)} %shard_map.105.refs_1_, bf16[16,40,128]{2,1,0:T(8,128)(2,1)} %copy-done.4), custom_call_target="tpu_custom_call" | custom-call | flops 2000000000 | bytes 6000000 | tf_op jit(solution)/shard_map/pallas_call | solution.py:36
  (5 shorter events, 0.1 us)
Async XLA Ops:
  7.2 18.4 %copy-start.2 = (bf16[1,128,1536]{2,1,0:T(8,128)(2,1)S(1)}, bf16[1,128,1536]{2,1,0:T(8,128)(2,1)}, u32[]{:S(2)}) copy-start(bf16[1,128,1536]{2,1,0:T(8,128)(2,1)} %param.8) | copy-start | bytes 1179652
  7.2 18.4 %copy-start.3 = (bf16[1,128,1536]{2,1,0:T(8,128)(2,1)S(1)}, bf16[1,128,1536]{2,1,0:T(8,128)(2,1)}, u32[]{:S(2)}) copy-start(bf16[1,128,1536]{2,1,0:T(8,128)(2,1)} %param.9) | copy-start | bytes 1179652
  7.2 56.6 %all-gather.7.cloned.1.call-start = ((), (), s32[]{:S(2)}) async-start(), calls=%async_computation.5 | async-start | bytes 3538944 | tf_op jit(solution)/shard_map/all_gather | solution.py:276
  7.9 23.8 %copy-start.5 = (s32[1,3,32]{2,0,1:T(1,128)S(1)}, s32[1,3,32]{2,0,1:T(1,128)}, u32[]{:S(2)}) copy-start(s32[1,3,32]{2,0,1:T(1,128)} %param.12) | copy-start | bytes 1156
  9.8 50.8 %all-to-all-start = ((bf16[16,144,128]{2,1,0:T(8,128)(2,1)}), bf16[16,144,128]{2,1,0:T(8,128)(2,1)S(1)}, u32[]{:S(2)}, u32[]{:S(2)}) async-start(bf16[16,144,128]{2,1,0:T(8,128)(2,1)} %shard_map.101.refs_1_), calls=%async_computation | async-start | bytes 1179648 | tf_op jit(solution)/shard_map/all_to_all | solution.py:285
  25.5 99.7 %all-gather.5.cloned.1.call-start = ((), (), s32[]{:S(2)}) async-start(), calls=%async_computation.4 | async-start | bytes 5308416 | tf_op jit(solution)/shard_map/all_gather | solution.py:301
  25.7 27.6 %collective-permute-start = (bf16[2,64,1536]{2,1,0:T(8,128)(2,1)S(1)}, bf16[2,64,1536]{2,1,0:T(8,128)(2,1)S(1)}, u32[]{:S(2)}, u32[]{:S(2)}) collective-permute-start(bf16[2,64,1536]{2,1,0:T(8,128)(2,1)S(1)} %pad_maximum_fusion), channel_id=1, source_target_pairs={{0,64},{64,128},{128,192},{192,256},{256,320},{320,384},{384,448},... | collective-permute-start | bytes 1179656 | tf_op jit(solution)/shard_map/ppermute | solution.py:277
  29.8 23.5 %collective-permute-start.1 = (bf16[2,64,1536]{2,1,0:T(8,128)(2,1)S(1)}, bf16[2,64,1536]{2,1,0:T(8,128)(2,1)S(1)}, u32[]{:S(2)}, u32[]{:S(2)}) collective-permute-start(bf16[2,64,1536]{2,1,0:T(8,128)(2,1)S(1)} %pad_maximum_fusion.1), channel_id=1, source_target_pairs={{64,0},{128,64},{192,128},{256,192},{320,256},{384,320},{448,384},... | collective-permute-start | bytes 1179656 | tf_op jit(solution)/shard_map/ppermute | solution.py:278
  53.3 0.7 copy-start.6
  53.3 0.9 copy-start.7
  60.5 0.9 copy-start
  89.7 12.2 %all-to-all-start.2 = ((bf16[4,576,128]{2,1,0:T(8,128)(2,1)}), bf16[4,576,128]{2,1,0:T(8,128)(2,1)S(1)}, u32[]{:S(2)}, u32[]{:S(2)}) async-start(bf16[4,576,128]{2,1,0:T(8,128)(2,1)} %shard_map.108), calls=%async_computation.2 | async-start | bytes 1179648 | tf_op jit(solution)/shard_map/all_to_all | solution.py:329
  102.0 0.8 copy-start.1
  104.7 17.1 %collective-permute-start.2 = (bf16[2,64,1536]{2,1,0:T(8,128)(2,1)}, bf16[2,64,1536]{2,1,0:T(8,128)(2,1)S(1)}, u32[]{:S(2)}, u32[]{:S(2)}) collective-permute-start(bf16[2,64,1536]{2,1,0:T(8,128)(2,1)} %shard_map.110), channel_id=1, source_target_pairs={{0,64},{64,128},{128,192},{192,256},{256,320},{320,384},{384,448},... | collective-permute-start | bytes 1179656 | tf_op jit(solution)/shard_map/ppermute | solution.py:332
  109.5 12.2 %collective-permute-start.3 = (bf16[2,64,1536]{2,1,0:T(8,128)(2,1)}, bf16[2,64,1536]{2,1,0:T(8,128)(2,1)S(1)}, u32[]{:S(2)}, u32[]{:S(2)}) collective-permute-start(bf16[2,64,1536]{2,1,0:T(8,128)(2,1)} %shard_map.111), channel_id=1, source_target_pairs={{64,0},{128,64},{192,128},{256,192},{320,256},{384,320},{448,384},... | collective-permute-start | bytes 1179656 | tf_op jit(solution)/shard_map/ppermute | solution.py:333
  111.4 24.1 %all-to-all-start.3 = ((bf16[16,40,128]{2,1,0:T(8,128)(2,1)}), bf16[16,40,128]{2,1,0:T(8,128)(2,1)S(1)}, u32[]{:S(2)}, u32[]{:S(2)}) async-start(bf16[16,40,128]{2,1,0:T(8,128)(2,1)} %shard_map.109.refs_1_), calls=%async_computation.3 | async-start | bytes 327680 | tf_op jit(solution)/shard_map/all_to_all | solution.py:331
  121.8 0.7 copy-start.8
  121.8 0.9 copy-start.9
  135.6 0.7 copy-start.4
Sparse Core Ops, SparseCore 0:
  10.1 43.3 all-gather.6
  63.9 41.5 all-gather.4

commit v4 on v3

--- a/solution.py
+++ b/solution.py
@@ -329,12 +329,12 @@
     term = lax.all_to_all(term, "dp", split_axis=0, concat_axis=0, tiled=True)
     summed = call(sum_kernel, shape((fsdp_size, columns + 16, 128), BF16), (term,), after=(to_left,))
     term = lax.all_to_all(summed, "fsdp", split_axis=0, concat_axis=0, tiled=True)
-    from_left = lax.ppermute(held_until(to_right, (summed,)), "seq", upward)
-    from_right = lax.ppermute(held_until(to_left, (summed,)), "seq", downward)
+    layer_out = call(layer_kernel, shape((tokens, model), BF16), (attended, full_weight), us=4, after=(summed,))
+    from_left = lax.ppermute(held_until(to_right, (layer_out,)), "seq", upward)
+    from_right = lax.ppermute(held_until(to_left, (layer_out,)), "seq", downward)
     key_grad, value_grad = call(
         finish_kernel, (shape((tokens, model), BF16),) * 2, (key_own, value_own, from_left, from_right)
     )
-    layer_out = call(layer_kernel, shape((tokens, model), BF16), (attended, full_weight), us=4)
     weight_grad = call(
         functools.partial(mean_kernel, clips=fsdp_size * dp_size),
         shape((columns, width), F32),

time: 146 us -> 141 us (0.966)
  blocking collectives: 38.1 us -> 34.3 us
    all_to_all x1, waiting for transfers between devices: 6.38 us -> 0.01 us  [per_device(): lax.all_to_all(summed, 'fsdp', split_axis=0, concat_axis=0, tiled=True)]
    ppermute x2, waiting for transfers between devices: 0.01 us -> 5.01 us  [the longest x1 4.01 us: per_device(): lax.ppermute(held_until(to_left, (layer_out,)), 'seq', downward)]
    all_gather x1, blocking collectives: 20.3 us -> 17.1 us  [per_device(): counts = lax.all_gather(own_count, 'seq', axis=0, tiled=True)]
  transfers between devices with their start and end apart: 9 -> 9, of which waited for: 2 -> 3; matrix products, arithmetic and copies ran while one was open for 1% -> 1% of each run, Pallas kernels for 24% -> 24%
where the time goes in v4:
time: 141 us; the launch traced here: 140 us
  starting transfers between devices  44.3 us (31%)
  Pallas kernels  35.7 us (25%)
  blocking collectives  34.3 us (24%)
  between operations  14.2 us (10%)
  waiting for transfers between devices  6.56 us (5%)
  local copies, waits for them, and re-layouts  5.24 us (4%)
    pallas_call x10, Pallas kernels, call(): pl.pallas_call(body, out_shape=out_shape, in_specs=[pl.BlockSpec(memory_s...  35.7 us
    all_to_all x1, blocking collectives, per_device(): lax.all_to_all(mixed, 'seq', split_axis=0, concat_axis=0, tiled=True)  17.2 us
    all_gather x1, blocking collectives, per_device(): counts = lax.all_gather(own_count, 'seq', axis=0, tiled=True)  17.1 us
    all_to_all x1, starting transfers between devices, per_device(): lax.all_to_all(weight_copies, 'fsdp', split_axis=0, concat_axis=0, tiled=...  15.7 us
    all_to_all x1, starting transfers between devices, per_device(): lax.all_to_all(summed, 'fsdp', split_axis=0, concat_axis=0, tiled=True)  10.9 us
    unnamed x22, local copies, waits for them, and re-layouts  5.19 us
    ppermute x1, starting transfers between devices, per_device(): lax.ppermute(held_until(to_left, (layer_out,)), 'seq', downward)  5.05 us
    all_to_all x1, starting transfers between devices, per_device(): term = lax.all_to_all(term, 'dp', split_axis=0, concat_axis=0, tiled=True)  4.43 us
  transfers between devices with their start and end apart: 9, of which 3 were waited for; matrix products, arithmetic and copies ran while one was open for 1% of the time, Pallas kernels for 24%

profile of v4, /device:TPU:1, one launch (start us, length us, event | category | flops | bytes accessed | tf_op | source)
XLA Modules:
  0.0 140.5 jit_solution(14832300772867276717)
XLA Ops:
  7.2 0.0 copy-start.2
  7.2 0.0 copy-start.3
  7.2 0.0 all-gather.7.cloned.1.call-start
  7.2 0.7 all-gather.7.cloned.1.call-update
  7.9 0.0 copy-start.5
  7.9 1.8 %shard_map.101.refs_1_ = bf16[16,144,128]{2,1,0:T(8,128)(2,1)} custom-call(bf16[192,96]{1,0:T(8,128)(2,1)} %refs_0_.1), custom_call_target="tpu_custom_call" | custom-call | flops 2000000000 | bytes 6000000 | tf_op jit(solution)/shard_map/pallas_call | solution.py:36
  9.8 15.7 %all-to-all-start = ((bf16[16,144,128]{2,1,0:T(8,128)(2,1)}), bf16[16,144,128]{2,1,0:T(8,128)(2,1)S(1)}, u32[]{:S(2)}, u32[]{:S(2)}) async-start(bf16[16,144,128]{2,1,0:T(8,128)(2,1)} %shard_map.101.refs_1_), calls=%async_computation | async-start | bytes 1179648 | tf_op jit(solution)/shard_map/all_to_all | solution.py:285
  25.5 0.0 all-gather.5.cloned.1.call-start
  25.6 0.0 copy-done.2
  25.6 0.0 copy-done.3
  25.6 0.1 fusion
  25.7 2.9 %collective-permute-start.1 = (bf16[2,64,1536]{2,1,0:T(8,128)(2,1)S(1)}, bf16[2,64,1536]{2,1,0:T(8,128)(2,1)S(1)}, u32[]{:S(2)}, u32[]{:S(2)}) collective-permute-start(bf16[2,64,1536]{2,1,0:T(8,128)(2,1)S(1)} %pad_maximum_fusion.1), channel_id=1, source_target_pairs={{64,0},{128,64},{192,128},{256,192},{320,256},{384,320},{448,384},... | collective-permute-start | bytes 1179656 | tf_op jit(solution)/shard_map/ppermute | solution.py:278
  28.6 3.1 %collective-permute-start = (bf16[2,64,1536]{2,1,0:T(8,128)(2,1)S(1)}, bf16[2,64,1536]{2,1,0:T(8,128)(2,1)S(1)}, u32[]{:S(2)}, u32[]{:S(2)}) collective-permute-start(bf16[2,64,1536]{2,1,0:T(8,128)(2,1)S(1)} %pad_maximum_fusion), channel_id=1, source_target_pairs={{0,64},{64,128},{128,192},{192,256},{256,320},{320,384},{384,448},... | collective-permute-start | bytes 1179656 | tf_op jit(solution)/shard_map/ppermute | solution.py:277
  31.7 0.0 copy-done.5
  31.7 0.6 copy.16
  32.3 17.1 %all-gather.1 = s32[8,3,32]{2,1,0:T(4,128)S(1)} all-gather(s32[1,3,32]{2,1,0:T(4,128)} %bitcast.20), channel_id=1, replica_groups=mesh['seq'=8,'fsdp'=16,'dp'=4] {'seq'}, dimensions={0}, use_global_device_ids=true | all-gather | bytes 3456 | tf_op jit(solution)/shard_map/all_gather | solution.py:286
  49.4 0.6 reshape.24.refs_0_
  50.0 0.0 collective-permute-done.1.refs_6_
  50.0 0.0 copy-start.6
  50.1 0.0 collective-permute-done.refs_5_
  50.1 0.0 copy-start.7
  50.1 0.7 copy-done.6
  50.8 0.1 copy-done.7
  50.9 6.4 %shard_map.103 = (bf16[1536,128]{1,0:T(8,128)(2,1)}, f32[12,1,256]{2,1,0:T(1,128)}) custom-call(s32[24,32]{1,0:T(8,128)} %reshape.24.refs_0_, s32[1]{0:T(128)} %bitcast.1.refs_1_, bf16[128,1536]{1,0:T(8,128)(2,1)} %bitcast.23, bf16[128,1536]{1,0:T(8,128)(2,1)} %bitcast.15, bf16[128,1536]{1,0:T(8,128)(2,1)} %bitcast.17, bf16[2,64,1536]{2,1,0:T(8,128)(2,1)} %copy-done.7, ...), custom_call_target="tpu_custom_call" | custom-call | flops 7000000000 | bytes 21000000 | tf_op jit(solution)/shard_map/pallas_call | solution.py:36
  57.3 0.0 all-to-all-done.refs_1_
  57.3 0.0 copy-start
  57.3 0.9 copy-done
  58.2 2.4 %shard_map.104.refs_0_ = bf16[192,1536]{1,0:T(8,128)(2,1)} custom-call(f32[12,1,256]{2,1,0:T(1,128)} %get-tuple-element.15.refs_0_.refs_8_, bf16[16,144,128]{2,1,0:T(8,128)(2,1)} %copy-done), custom_call_target="tpu_custom_call" | custom-call | flops 2000000000 | bytes 6000000 | tf_op jit(solution)/shard_map/pallas_call | solution.py:36
  60.6 0.0 all-gather.5.cloned.1.call-update
  60.6 0.0 all-gather.7.cloned.1.call-done
  60.7 4.1 %shard_map.105 = bf16[8,384,128]{2,1,0:T(8,128)(2,1)} custom-call(bf16[192,1536]{1,0:T(8,128)(2,1)} %shard_map.104.refs_0_, bf16[1024,1536]{1,0:T(8,128)(2,1)} %bitcast.21, bf16[1536,128]{1,0:T(8,128)(2,1)} %get-tuple-element.14.refs_2_.refs_7_.refs_1_), custom_call_target="tpu_custom_call" | custom-call | flops 4000000000 | bytes 12000000 | tf_op jit(solution)/shard_map/pallas_call | solution.py:36
  64.7 17.2 %all_to_all.20.refs_9_.refs_0_ = bf16[8,384,128]{2,1,0:T(8,128)(2,1)} all-to-all(bf16[8,384,128]{2,1,0:T(8,128)(2,1)} %shard_map.105), channel_id=1, replica_groups=mesh['seq'=8,'fsdp'=16,'dp'=4] {'seq'}, dimensions={0} | all-to-all | bytes 1572864 | tf_op jit(solution)/shard_map/all_to_all | solution.py:308
  82.0 3.9 %shard_map.107 = bf16[4,576,128]{2,1,0:T(8,128)(2,1)} custom-call(bf16[8,384,128]{2,1,0:T(8,128)(2,1)} %all_to_all.20.refs_9_.refs_0_, bf16[1024,1536]{1,0:T(8,128)(2,1)} %bitcast.22), custom_call_target="tpu_custom_call" | custom-call | flops 4000000000 | bytes 12000000 | tf_op jit(solution)/shard_map/pallas_call | solution.py:36
  85.9 4.4 %all-to-all-start.2 = ((bf16[4,576,128]{2,1,0:T(8,128)(2,1)}), bf16[4,576,128]{2,1,0:T(8,128)(2,1)S(1)}, u32[]{:S(2)}, u32[]{:S(2)}) async-start(bf16[4,576,128]{2,1,0:T(8,128)(2,1)} %shard_map.107), calls=%async_computation.2 | async-start | bytes 1179648 | tf_op jit(solution)/shard_map/all_to_all | solution.py:329
  90.3 7.0 %shard_map.106 = (bf16[128,1536]{1,0:T(8,128)(2,1)}, f32[128,1536]{1,0:T(8,128)}, f32[128,1536]{1,0:T(8,128)}, bf16[2,64,1536]{2,1,0:T(8,128)(2,1)}, bf16[2,64,1536]{2,1,0:T(8,128)(2,1)}) custom-call(s32[24,32]{1,0:T(8,128)} %reshape.24.refs_0_, s32[1]{0:T(128)} %bitcast.1.refs_1_, bf16[128,1536]{1,0:T(8,128)(2,1)} %bitcast.24, bf16[128,1536]{1,0:T(8,128)(2,1)} %bitcast.16, ...), custom_call_target="tpu_custom_call" | custom-call | flops 7000000000 | bytes 21000000 | tf_op jit(solution)/shard_map/pallas_call | solution.py:36
  97.4 0.8 all-to-all-done.2.refs_1_
  98.2 0.0 copy-start.1
  98.2 0.8 copy-done.1
  99.0 1.9 %shard_map.108.refs_0_ = bf16[16,40,128]{2,1,0:T(8,128)(2,1)} custom-call(bf16[2,64,1536]{2,1,0:T(8,128)(2,1)} %get-tuple-element.16.refs_0_, bf16[4,576,128]{2,1,0:T(8,128)(2,1)} %copy-done.1), custom_call_target="tpu_custom_call" | custom-call | flops 2000000000 | bytes 6000000 | tf_op jit(solution)/shard_map/pallas_call | solution.py:36
  100.9 10.9 %all-to-all-start.3 = ((bf16[16,40,128]{2,1,0:T(8,128)(2,1)}), bf16[16,40,128]{2,1,0:T(8,128)(2,1)S(1)}, u32[]{:S(2)}, u32[]{:S(2)}) async-start(bf16[16,40,128]{2,1,0:T(8,128)(2,1)} %shard_map.108.refs_0_), calls=%async_computation.3 | async-start | bytes 327680 | tf_op jit(solution)/shard_map/all_to_all | solution.py:331
  111.8 0.0 all-gather.5.cloned.1.call-done.refs_2_
  111.8 4.0 %shard_map.109.refs_1_ = bf16[128,1536]{1,0:T(8,128)(2,1)} custom-call(bf16[16,40,128]{2,1,0:T(8,128)(2,1)} %shard_map.108.refs_0_, bf16[1536,128]{1,0:T(8,128)(2,1)} %get-tuple-element.14.refs_2_.refs_7_.refs_1_, bf16[1536,1536]{1,0:T(8,128)(2,1)} %all-gather.5.cloned.1.call-done.refs_2_), custom_call_target="tpu_custom_call" | custom-call | flops 4000000000 | bytes 12000000 | tf_op jit(solution)/shard_map/pallas_call | solution.py:36
  115.8 5.0 %collective-permute-start.3 = (bf16[2,64,1536]{2,1,0:T(8,128)(2,1)}, bf16[2,64,1536]{2,1,0:T(8,128)(2,1)S(1)}, u32[]{:S(2)}, u32[]{:S(2)}) collective-permute-start(bf16[2,64,1536]{2,1,0:T(8,128)(2,1)} %shard_map.111), channel_id=1, source_target_pairs={{64,0},{128,64},{192,128},{256,192},{320,256},{384,320},{448,384},... | collective-permute-start | bytes 1179656 | tf_op jit(solution)/shard_map/ppermute | solution.py:334
  120.9 2.1 %collective-permute-start.2 = (bf16[2,64,1536]{2,1,0:T(8,128)(2,1)}, bf16[2,64,1536]{2,1,0:T(8,128)(2,1)S(1)}, u32[]{:S(2)}, u32[]{:S(2)}) collective-permute-start(bf16[2,64,1536]{2,1,0:T(8,128)(2,1)} %shard_map.110), channel_id=1, source_target_pairs={{0,64},{64,128},{128,192},{192,256},{256,320},{320,384},{384,448},... | collective-permute-start | bytes 1179656 | tf_op jit(solution)/shard_map/ppermute | solution.py:333
  123.0 4.0 %collective-permute-done.3.refs_3_ = bf16[2,64,1536]{2,1,0:T(8,128)(2,1)S(1)} collective-permute-done((bf16[2,64,1536]{2,1,0:T(8,128)(2,1)}, bf16[2,64,1536]{2,1,0:T(8,128)(2,1)S(1)}, u32[]{:S(2)}, u32[]{:S(2)}) %collective-permute-start.3) | collective-permute-done | bytes 393248 | tf_op jit(solution)/shard_map/ppermute | solution.py:334
  127.1 0.0 copy-start.8
  127.1 1.0 collective-permute-done.2.refs_2_
  128.1 0.0 copy-start.9
  128.1 0.0 copy-done.8
  128.1 0.7 copy-done.9
  128.8 2.5 %shard_map.112 = (bf16[128,1536]{1,0:T(8,128)(2,1)}, bf16[128,1536]{1,0:T(8,128)(2,1)}) custom-call(f32[128,1536]{1,0:T(8,128)} %get-tuple-element.18.refs_0_, f32[128,1536]{1,0:T(8,128)} %get-tuple-element.19.refs_1_, bf16[2,64,1536]{2,1,0:T(8,128)(2,1)} %copy-done.9, bf16[2,64,1536]{2,1,0:T(8,128)(2,1)} %copy-done.8), custom_call_target="tpu_custom_call" | custom-call | flops 2000000000 | bytes 6000000 | tf_op jit(solution)/shard_map/pallas_call | solution.py:36
  131.3 0.0 all-to-all-done.3.refs_2_
  131.3 0.0 copy-start.4
  131.3 0.7 copy-done.4
  132.0 1.6 %shard_map.113 = f32[24,192]{1,0:T(8,128)} custom-call(bf16[128,1536]{1,0:T(8,128)(2,1)} %get-tuple-element.21.refs_0_, bf16[128,1536]{1,0:T(8,128)(2,1)} %shard_map.109.refs_1_, bf16[16,40,128]{2,1,0:T(8,128)(2,1)} %copy-done.4), custom_call_target="tpu_custom_call" | custom-call | flops 2000000000 | bytes 6000000 | tf_op jit(solution)/shard_map/pallas_call | solution.py:36
  (5 shorter events, 0.1 us)
Async XLA Ops:
  7.2 18.4 %copy-start.2 = (bf16[1,128,1536]{2,1,0:T(8,128)(2,1)S(1)}, bf16[1,128,1536]{2,1,0:T(8,128)(2,1)}, u32[]{:S(2)}) copy-start(bf16[1,128,1536]{2,1,0:T(8,128)(2,1)} %param.8) | copy-start | bytes 1179652
  7.2 18.4 %copy-start.3 = (bf16[1,128,1536]{2,1,0:T(8,128)(2,1)S(1)}, bf16[1,128,1536]{2,1,0:T(8,128)(2,1)}, u32[]{:S(2)}) copy-start(bf16[1,128,1536]{2,1,0:T(8,128)(2,1)} %param.9) | copy-start | bytes 1179652
  7.2 53.5 %all-gather.7.cloned.1.call-start = ((), (), s32[]{:S(2)}) async-start(), calls=%async_computation.5 | async-start | bytes 3538944 | tf_op jit(solution)/shard_map/all_gather | solution.py:276
  7.9 23.8 %copy-start.5 = (s32[1,3,32]{2,0,1:T(1,128)S(1)}, s32[1,3,32]{2,0,1:T(1,128)}, u32[]{:S(2)}) copy-start(s32[1,3,32]{2,0,1:T(1,128)} %param.12) | copy-start | bytes 1156
  9.8 47.6 %all-to-all-start = ((bf16[16,144,128]{2,1,0:T(8,128)(2,1)}), bf16[16,144,128]{2,1,0:T(8,128)(2,1)S(1)}, u32[]{:S(2)}, u32[]{:S(2)}) async-start(bf16[16,144,128]{2,1,0:T(8,128)(2,1)} %shard_map.101.refs_1_), calls=%async_computation | async-start | bytes 1179648 | tf_op jit(solution)/shard_map/all_to_all | solution.py:285
  25.5 86.3 %all-gather.5.cloned.1.call-start = ((), (), s32[]{:S(2)}) async-start(), calls=%async_computation.4 | async-start | bytes 5308416 | tf_op jit(solution)/shard_map/all_gather | solution.py:301
  25.7 24.4 %collective-permute-start.1 = (bf16[2,64,1536]{2,1,0:T(8,128)(2,1)S(1)}, bf16[2,64,1536]{2,1,0:T(8,128)(2,1)S(1)}, u32[]{:S(2)}, u32[]{:S(2)}) collective-permute-start(bf16[2,64,1536]{2,1,0:T(8,128)(2,1)S(1)} %pad_maximum_fusion.1), channel_id=1, source_target_pairs={{64,0},{128,64},{192,128},{256,192},{320,256},{384,320},{448,384},... | collective-permute-start | bytes 1179656 | tf_op jit(solution)/shard_map/ppermute | solution.py:278
  28.6 21.5 %collective-permute-start = (bf16[2,64,1536]{2,1,0:T(8,128)(2,1)S(1)}, bf16[2,64,1536]{2,1,0:T(8,128)(2,1)S(1)}, u32[]{:S(2)}, u32[]{:S(2)}) collective-permute-start(bf16[2,64,1536]{2,1,0:T(8,128)(2,1)S(1)} %pad_maximum_fusion), channel_id=1, source_target_pairs={{0,64},{64,128},{128,192},{192,256},{256,320},{320,384},{384,448},... | collective-permute-start | bytes 1179656 | tf_op jit(solution)/shard_map/ppermute | solution.py:277
  50.0 0.7 copy-start.6
  50.1 0.9 copy-start.7
  57.3 0.9 copy-start
  85.9 12.3 %all-to-all-start.2 = ((bf16[4,576,128]{2,1,0:T(8,128)(2,1)}), bf16[4,576,128]{2,1,0:T(8,128)(2,1)S(1)}, u32[]{:S(2)}, u32[]{:S(2)}) async-start(bf16[4,576,128]{2,1,0:T(8,128)(2,1)} %shard_map.107), calls=%async_computation.2 | async-start | bytes 1179648 | tf_op jit(solution)/shard_map/all_to_all | solution.py:329
  98.2 0.8 copy-start.1
  100.9 30.5 %all-to-all-start.3 = ((bf16[16,40,128]{2,1,0:T(8,128)(2,1)}), bf16[16,40,128]{2,1,0:T(8,128)(2,1)S(1)}, u32[]{:S(2)}, u32[]{:S(2)}) async-start(bf16[16,40,128]{2,1,0:T(8,128)(2,1)} %shard_map.108.refs_0_), calls=%async_computation.3 | async-start | bytes 327680 | tf_op jit(solution)/shard_map/all_to_all | solution.py:331
  115.8 11.2 %collective-permute-start.3 = (bf16[2,64,1536]{2,1,0:T(8,128)(2,1)}, bf16[2,64,1536]{2,1,0:T(8,128)(2,1)S(1)}, u32[]{:S(2)}, u32[]{:S(2)}) collective-permute-start(bf16[2,64,1536]{2,1,0:T(8,128)(2,1)} %shard_map.111), channel_id=1, source_target_pairs={{64,0},{128,64},{192,128},{256,192},{320,256},{384,320},{448,384},... | collective-permute-start | bytes 1179656 | tf_op jit(solution)/shard_map/ppermute | solution.py:334
  120.9 7.2 %collective-permute-start.2 = (bf16[2,64,1536]{2,1,0:T(8,128)(2,1)}, bf16[2,64,1536]{2,1,0:T(8,128)(2,1)S(1)}, u32[]{:S(2)}, u32[]{:S(2)}) collective-permute-start(bf16[2,64,1536]{2,1,0:T(8,128)(2,1)} %shard_map.110), channel_id=1, source_target_pairs={{0,64},{64,128},{128,192},{192,256},{256,320},{320,384},{384,448},... | collective-permute-start | bytes 1179656 | tf_op jit(solution)/shard_map/ppermute | solution.py:333
  127.1 1.0 copy-start.8
  128.1 0.8 copy-start.9
  131.3 0.7 copy-start.4
Sparse Core Ops, SparseCore 0:
  10.1 42.8 all-gather.6
  60.7 41.8 all-gather.4
